TPU v7x, 32 devices: a whole 2x2x4 slice. The times are simulated.
32 devices in a mesh: seq: 8 (over z, x), mp: 4 (over y, core).
Axes of the slice: x: 2, y: 2, z: 4, core: 2. Of those that a mesh axis runs over, the one named last changes fastest.
Arguments:
- hidden_in: bfloat16 [32, 2048], P('mp'), may hold values from -24 to 24
- query_weight: bfloat16 [2048, 3072], P(None, 'seq'), may hold values from -0.25 to 0.25
- key_absorb: bfloat16 [16, 128, 512], replicated, may hold values from -0.5 to 0.5
- value_up: bfloat16 [16, 512, 128], replicated, may hold values from -0.25 to 0.25
- out_weight: bfloat16 [2048, 2048], P(None, 'seq'), may hold values from -0.5 to 0.5
- latent_cache: bfloat16 [32, 1024, 576], P('mp', 'seq'), may hold values from -41 to 41
- cache_lengths: int32 [32], P('mp'), may hold values from 128 to 1024, as said below
- keep_lists: int32 [32, 8, 64], P('mp', 'seq'), may hold values from 0 to 127, as said below
- drop_weights: int32 [32, 1024], P('mp', 'seq'), may hold values from 1 to 8
- pack_dest: int32 [32, 8], P('mp'), may hold values from -1 to 31, as said below
- final_gain: bfloat16 [2048], replicated, may hold values from 0.5 to 1.5
- head_weight: bfloat16 [2048, 102400], P(None, ('seq', 'mp')), may hold values from -0.125 to 0.125
- tenant_ranges: int32 [4, 2], replicated, may hold values from 0 to 102400, as said below
- tenant_ids: int32 [32], replicated, may hold values from 0 to 3
Outputs:
- packed_rows: bfloat16 [128, 64, 576], P(('seq', 'mp'))
- packed_summary: bfloat16 [128, 576], P(('seq', 'mp'))
- hidden_out: bfloat16 [32, 2048], P('mp', 'seq')
- state_norm: float32 [32], P('mp')
- top_logit: float32 [32], P('mp')
Inputs may be any that keep to these rules, and one draw needn't show every extreme that they name: `cache_lengths`: every length is a whole number of 128-position blocks, at least one block. Within each group of 8 requests (one index of mp) the lengths add up to 4096, and some request of the group has the full 1024. `keep_lists`: the 64 positions of a block are distinct and ascending. pack_dest[r, b] is -1 exactly when block b of request r is not live; otherwise it is owner * 4 + slot with an owner in 0 to 8 - 1 (an index of seq) and a slot in 0 to 3. Within one group of 8 requests the live blocks take every destination exactly once. Of the live blocks of one block index in one group, at most 1 go to any one owner, and those that share an owner take consecutive slots. Block index 0 is live for every request of a group, and some owner receives 1 of them. `tenant_ranges`: row t is tenant t's window [low, high) of vocabulary entries; each window holds at least 51200 entries.
All inputs are finite; a program needn't handle non-finite values.
Results may differ from a plain program's by a relative error of at most 0.0075.
Values may be sent and summed in bfloat16 or wider, within the bound.
A program may use at most 128 MiB of HBM per device.

v0:
```python
import jax
import jax.numpy as jnp
from jax import lax
from jax.sharding import PartitionSpec as P

H = 16
NOPE = 128
ROPE = 64
LAT = 512
VH = 128
BLK = 128
KB = 64
TENANTS = 4
RQ = 8


NEGATIVE = -1e30
HIGHEST = lax.Precision.HIGHEST


def merged(x, axis, combine):
    everything = jax.tree.map(lambda part: lax.all_gather(part, axis), x)
    initial = jax.tree.map(lambda part: part[0], everything)

    def step(k, so_far):
        return combine(so_far, jax.tree.map(lambda part: part[k], everything))

    return lax.fori_loop(1, lax.axis_size(axis), step, initial)


def compact_blocks(block_rows, keep_onehot, weights_dropped):
    kept_rows = jnp.einsum(
        "nkt,ntc->nkc", keep_onehot, block_rows, preferred_element_type=jnp.float32
    ).astype(jnp.bfloat16)
    weight_mass = jnp.sum(weights_dropped.astype(jnp.float32), axis=1)
    summed = jnp.einsum(
        "nt,ntc->nc", weights_dropped, block_rows, preferred_element_type=jnp.float32
    )
    summary = (summed / weight_mass[:, None]).astype(jnp.bfloat16)
    return (kept_rows, summary)


def attend_blocks(query_lat, query_rope, kept_rows, summary, usable):
    score_scale = (NOPE + ROPE) ** (-0.5)
    row_scores = (
        jnp.einsum(
            "nhl,nkl->nhk", query_lat, kept_rows[:, :, :LAT], preferred_element_type=jnp.float32
        )
        + jnp.einsum(
            "nhr,nkr->nhk", query_rope, kept_rows[:, :, LAT:], preferred_element_type=jnp.float32
        )
    ) * score_scale
    summ_scores = (
        jnp.einsum("nhl,nl->nh", query_lat, summary[:, :LAT], preferred_element_type=jnp.float32)
        + jnp.einsum("nhr,nr->nh", query_rope, summary[:, LAT:], preferred_element_type=jnp.float32)
    ) * score_scale
    summ_scores = summ_scores + jnp.log(jnp.float32(BLK - KB))
    row_scores = jnp.where(usable[:, None, None], row_scores, NEGATIVE)
    summ_scores = jnp.where(usable[:, None], summ_scores, NEGATIVE)
    maxima = jnp.maximum(jnp.max(row_scores, axis=2), summ_scores)
    row_weights = jnp.where(usable[:, None, None], jnp.exp(row_scores - maxima[:, :, None]), 0.0)
    summ_weights = jnp.where(usable[:, None], jnp.exp(summ_scores - maxima), 0.0)
    totals = jnp.sum(row_weights, axis=2) + summ_weights
    weighted = jnp.einsum(
        "nhk,nkl->nhl", row_weights, kept_rows[:, :, :LAT].astype(jnp.float32), precision=HIGHEST
    )
    weighted = weighted + summ_weights[:, :, None] * summary[:, None, :LAT].astype(jnp.float32)
    return (maxima, totals, weighted)


def per_request(maxima, totals, weighted, owner_of):
    request_max = jnp.max(jnp.where(owner_of[:, :, None], maxima[None, :, :], NEGATIVE), axis=1)
    shifted = jnp.where(owner_of[:, :, None], maxima[None, :, :] - request_max[:, None, :], 0.0)
    factor = jnp.where(owner_of[:, :, None], jnp.exp(shifted), 0.0)
    request_total = jnp.einsum("rnh,nh->rh", factor, totals, precision=HIGHEST)
    request_sum = jnp.einsum("rnh,nhl->rhl", factor, weighted, precision=HIGHEST)
    return (request_max, request_total, request_sum)


def combine_partial(former, latter):
    former_max, former_total, former_sum = former
    latter_max, latter_total, latter_sum = latter
    joined = jnp.maximum(former_max, latter_max)
    former_factor = jnp.exp(former_max - joined)
    latter_factor = jnp.exp(latter_max - joined)
    return (
        joined,
        former_factor * former_total + latter_factor * latter_total,
        former_factor[:, :, None] * former_sum + latter_factor[:, :, None] * latter_sum,
    )


def body(
    hidden_in,
    query_weight,
    key_absorb,
    value_up,
    out_weight,
    latent_cache,
    cache_lengths,
    keep_lists,
    drop_weights,
    pack_dest,
    final_gain,
    head_weight,
    tenant_ranges,
    tenant_ids,
):
    seq_count = lax.axis_size("seq")
    mp_count = lax.axis_size("mp")
    seq_index = lax.axis_index("seq")
    mp_index = lax.axis_index("mp")
    capacity = max(1, RQ // seq_count)
    slot_count = RQ // 2
    row_width = LAT + ROPE
    query_part = jnp.dot(hidden_in, query_weight, preferred_element_type=jnp.float32).astype(
        jnp.bfloat16
    )
    query_full = lax.all_gather(query_part, "seq", axis=1, tiled=True).reshape(RQ, H, NOPE + ROPE)
    query_lat = jnp.einsum(
        "rhn,hnl->rhl", query_full[:, :, :NOPE], key_absorb, preferred_element_type=jnp.float32
    ).astype(jnp.bfloat16)
    query_rope = query_full[:, :, NOPE:]
    positions = jnp.arange(BLK, dtype=jnp.int32)
    keep_onehot = keep_lists[:, 0, :, None] == positions[None, None, :]
    kept_flag = jnp.sum(keep_onehot.astype(jnp.int32), axis=1)
    weights_dropped = (drop_weights * (1 - kept_flag)).astype(jnp.bfloat16)
    live_here = cache_lengths > seq_index * BLK
    dest_here = lax.dynamic_slice_in_dim(pack_dest, seq_index, 1, 1)[:, 0]
    send_slot = dest_here // slot_count * capacity + dest_here % slot_count % capacity
    slot_range = jnp.arange(seq_count * capacity, dtype=jnp.int32)
    send_onehot = ((send_slot[None, :] == slot_range[:, None]) & live_here[None, :]).astype(
        jnp.bfloat16
    )
    targets = seq_index * slot_count + jnp.arange(slot_count, dtype=jnp.int32)
    slot_match = (pack_dest[None, :, :] == targets[:, None, None]).astype(jnp.int32)
    block_range = jnp.arange(pack_dest.shape[1], dtype=jnp.int32)
    source_of = jnp.sum(slot_match * block_range[None, None, :], axis=(1, 2))
    request_of = jnp.sum(slot_match, axis=2)
    request_index = jnp.sum(request_of * jnp.arange(RQ, dtype=jnp.int32)[None, :], axis=1)
    pick_index = source_of * capacity + jnp.arange(slot_count, dtype=jnp.int32) % capacity
    owner_of = jnp.transpose(request_of) > 0
    local_rows, local_summary = compact_blocks(
        latent_cache, keep_onehot.astype(jnp.bfloat16), weights_dropped
    )
    send_rows = jnp.einsum(
        "jr,rkc->jkc", send_onehot, local_rows, preferred_element_type=jnp.float32
    )
    send_rows = send_rows.astype(jnp.bfloat16).reshape(seq_count, capacity, KB, row_width)
    send_summary = jnp.dot(send_onehot, local_summary, preferred_element_type=jnp.float32)
    send_summary = send_summary.astype(jnp.bfloat16).reshape(seq_count, capacity, row_width)
    recv_rows, recv_summary = (
        lax.all_to_all(send_rows, "seq", split_axis=0, concat_axis=0, tiled=True),
        lax.all_to_all(send_summary, "seq", split_axis=0, concat_axis=0, tiled=True),
    )
    packed_rows = jnp.take(
        recv_rows.reshape(seq_count * capacity, KB, row_width), pick_index, axis=0
    )
    packed_summary = jnp.take(
        recv_summary.reshape(seq_count * capacity, row_width), pick_index, axis=0
    )
    slot_query_lat = jnp.take(query_lat, request_index, axis=0)
    slot_query_rope = jnp.take(query_rope, request_index, axis=0)
    usable = jnp.ones((slot_count,), dtype=bool)
    maxima, totals, weighted = attend_blocks(
        slot_query_lat, slot_query_rope, packed_rows, packed_summary, usable
    )
    partial_value = per_request(maxima, totals, weighted, owner_of)
    request_max, request_total, request_sum = merged(partial_value, "seq", combine_partial)
    attended = (request_sum / request_total[:, :, None]).astype(jnp.bfloat16)
    values = jnp.einsum("rhl,hlv->rhv", attended, value_up, preferred_element_type=jnp.float32)
    values = values.astype(jnp.bfloat16).reshape(RQ, H * VH)
    col_width = out_weight.shape[1]
    residual = lax.dynamic_slice_in_dim(hidden_in, seq_index * col_width, col_width, 1)
    hidden_out = (
        residual.astype(jnp.float32)
        + jnp.dot(values, out_weight, preferred_element_type=jnp.float32)
    ).astype(jnp.bfloat16)
    gathered = lax.all_gather(hidden_out[None], ("seq", "mp"), axis=0, tiled=True)
    all_rows = gathered.reshape(seq_count, mp_count, RQ, col_width).transpose(1, 2, 0, 3)
    all_rows = all_rows.reshape(mp_count * RQ, seq_count * col_width)
    rows_f = all_rows.astype(jnp.float32)
    mean_sq = jnp.mean(rows_f * rows_f, axis=1)
    norms_all = jnp.sqrt(mean_sq)
    normed = (
        rows_f * lax.rsqrt(mean_sq + 1e-06)[:, None] * final_gain.astype(jnp.float32)[None, :]
    ).astype(jnp.bfloat16)
    logits = jnp.dot(normed, head_weight, preferred_element_type=jnp.float32)
    vocab_width = head_weight.shape[1]
    device_index = seq_index * mp_count + mp_index
    columns = device_index * vocab_width + jnp.arange(vocab_width, dtype=jnp.int32)
    tenant_onehot = (tenant_ids[:, None] == jnp.arange(TENANTS, dtype=jnp.int32)[None, :]).astype(
        jnp.int32
    )
    window_low = jnp.sum(tenant_onehot * tenant_ranges[None, :, 0], axis=1)
    window_high = jnp.sum(tenant_onehot * tenant_ranges[None, :, 1], axis=1)
    allowed = (columns[None, :] >= window_low[:, None]) & (columns[None, :] < window_high[:, None])
    local_best = jnp.max(jnp.where(allowed, logits, NEGATIVE), axis=1)
    best_all = lax.pmax(local_best, ("seq", "mp"))
    row_start = mp_index * RQ
    state_norm = lax.dynamic_slice_in_dim(norms_all, row_start, RQ, 0)
    top_logit = lax.dynamic_slice_in_dim(best_all, row_start, RQ, 0)
    return (packed_rows, packed_summary, hidden_out, state_norm, top_logit)


def solution(mesh):
    in_specs = (
        P("mp", None),
        P(None, "seq"),
        P(),
        P(),
        P(None, "seq"),
        P("mp", "seq", None),
        P("mp"),
        P("mp", "seq", None),
        P("mp", "seq"),
        P("mp", None),
        P(),
        P(None, ("seq", "mp")),
        P(),
        P(),
    )
    out_specs = (
        P(("seq", "mp"), None, None),
        P(("seq", "mp"), None),
        P("mp", "seq"),
        P("mp"),
        P("mp"),
    )
    return jax.shard_map(body, mesh=mesh, in_specs=in_specs, out_specs=out_specs, check_vma=False)
```

profile of v0, /device:TPU:0, one launch (start us, length us, event | category | flops | bytes accessed | tf_op | source)
XLA Modules:
  0.0 248.3 jit_solution(1165486816989301828)
XLA Ops:
  7.2 1.0 dynamic-slice_reduce_fusion
  10.6 1.7 fusion.36
  14.4 7.3 %all-to-all-start.1 = ((bf16[8,2,288]{2,1,0:T(2,128)(2,1)}), bf16[8,2,288]{2,1,0:T(2,128)(2,1)S(1)}, u32[]{:S(2)}, u32[]{:S(2)}) async-start(bf16[8,2,288]{2,1,0:T(2,128)(2,1)} %reshape.210), calls=%async_computation.1 | async-start | bytes 24576 | tf_op jit(solution)/shard_map/all_to_all | solution.py:154
  21.6 2.1 convolution_convert_fusion.1
  24.2 1.6 fusion.4
  25.8 1.7 convolution_convert_fusion.5
  27.5 31.2 %all_gather.24 = bf16[8,3072]{1,0:T(8,128)(2,1)S(1)} all-gather(bf16[8,384]{1,0:T(8,128)(2,1)S(1)} %convolution_convert_fusion.5), channel_id=1, replica_groups=mesh['seq'=8,'mp'=4] {'seq'}, dimensions={1}, use_global_device_ids=true | all-gather | bytes 55296 | tf_op jit(solution)/shard_map/all_gather | solution.py:119
  61.4 5.4 %all-to-all-start = ((bf16[8,1,64,576]{3,2,1,0:T(8,128)(2,1)}), bf16[8,1,64,576]{3,2,1,0:T(8,128)(2,1)S(1)}, u32[]{:S(2)}, u32[]{:S(2)}) async-start(bf16[8,1,64,576]{3,2,1,0:T(8,128)(2,1)} %copy.91), calls=%async_computation | async-start | bytes 1310720 | tf_op jit(solution)/shard_map/all_to_all | solution.py:153
  68.0 10.5 %all-to-all-done = bf16[8,1,64,576]{3,2,1,0:T(8,128)(2,1)S(1)} async-done(((bf16[8,1,64,576]{3,2,1,0:T(8,128)(2,1)}), bf16[8,1,64,576]{3,2,1,0:T(8,128)(2,1)S(1)}, u32[]{:S(2)}, u32[]{:S(2)}) %all-to-all-start) | async-done | bytes 589856 | tf_op jit(solution)/shard_map/all_to_all | solution.py:153
  80.5 1.2 convolution_bitcast_fusion
  82.0 30.5 %all-gather = f32[64,16]{1,0:T(8,128)S(1)} all-gather(f32[8,16]{1,0:T(8,128)S(1)} %copy.96), channel_id=2, replica_groups=mesh['seq'=8,'mp'=4] {'seq'}, dimensions={0}, use_global_device_ids=true | all-gather | bytes 4608 | tf_op jit(solution)/shard_map/all_gather | solution.py:22
  112.8 30.6 %all-gather.1 = f32[64,16]{1,0:T(8,128)S(1)} all-gather(f32[8,16]{1,0:T(8,128)S(1)} %bitcast.106), channel_id=3, replica_groups=mesh['seq'=8,'mp'=4] {'seq'}, dimensions={0}, use_global_device_ids=true | all-gather | bytes 4608 | tf_op jit(solution)/shard_map/all_gather | solution.py:22
  144.6 8.6 %while.19 = (s32[]{:T(128)}, f32[8,16]{1,0:T(8,128)S(1)}, f32[8,16]{1,0:T(8,128)S(1)}, f32[8,16,512]{2,1,0:T(8,128)S(1)}, f32[8,8,16]{2,1,0:T(8,128)S(1)}, /*ind...) while((s32[]{:T(128)}, f32[8,16]{1,0:T(8,128)S(1)}, ...), condition=%wide.region_9.10_spmd, body=%wide.region_8.9_spmd.sunk | while | flops 197381 | bytes 1315991 | solution.py:28
  144.6 1.0 constant_dynamic-slice_fusion.2
  145.8 1.0 constant_dynamic-slice_fusion.2
  147.1 1.0 constant_dynamic-slice_fusion.2
  148.3 1.0 constant_dynamic-slice_fusion.2
  149.5 1.0 constant_dynamic-slice_fusion.2
  150.7 1.0 constant_dynamic-slice_fusion.2
  152.0 1.0 constant_dynamic-slice_fusion.2
  153.3 2.4 fusion.10
  155.7 40.0 %all-gather.3 = bf16[256,256]{1,0:T(8,128)(2,1)S(1)} all-gather(bf16[8,256]{1,0:T(8,128)(2,1)S(1)} %fusion.10), channel_id=5, replica_groups=mesh['seq'=8,'mp'=4] {'seq','mp'}, dimensions={0}, use_global_device_ids=true | all-gather | bytes 135168 | tf_op jit(solution)/shard_map/all_gather | solution.py:179
  196.2 7.2 %fusion.5 = f32[32]{0:T(128)S(1)} fusion(bf16[2048,3200]{1,0:T(8,128)(2,1)} %param.27, s32[3200]{0:T(1024)S(1)} %iota_add_fusion, s32[32]{0:T(128)S(1)} %get-tuple-element.241, s32[32]{0:T(128)S(1)} %get-tuple-element.240, f32[32,2048]{1,0:T(8,128)S(1)} %bitcast.95, f32[2048]{0:T(1024)S(1)} %convert_element_type.101, f32[32]{0:T(128)S(1)} %rsqrt.11), kind=kOutput, calls=%fused_computation.19 | convolution fusion | flops 420138976 | bytes 13390848 | tf_op jit(solution)/shard_map/dot_general | solution.py:188
  203.5 36.8 %pmax.7 = f32[32]{0:T(128)S(1)} all-reduce(f32[32]{0:T(128)S(1)} %fusion.5), channel_id=1, replica_groups=mesh['seq'=8,'mp'=4] {'seq','mp'}, use_global_device_ids=true, to_apply=%region_15.16 | all-reduce | flops 32 | bytes 256 | tf_op jit(solution)/shard_map/pmax | solution.py:199
  (104 shorter events, 15.5 us)
Async XLA Ops:
  7.2 51.7 %copy-start = (bf16[16,128,512]{2,1,0:T(8,128)(2,1)S(1)}, bf16[16,128,512]{2,1,0:T(8,128)(2,1)}, u32[]{:S(2)}) copy-start(bf16[16,128,512]{2,1,0:T(8,128)(2,1)} %param.18) | copy-start | bytes 6291460
  7.2 16.5 %copy-start.6 = (s32[8,8]{1,0:T(8,128)S(1)}, s32[8,8]{1,0:T(8,128)}, u32[]{:S(2)}) copy-start(s32[8,8]{1,0:T(8,128)} %param.25) | copy-start | bytes 772
  7.2 14.4 %copy-start.1 = (bf16[8,128,576]{1,2,0:T(8,128)(2,1)S(1)}, bf16[8,128,576]{1,2,0:T(8,128)(2,1)}, u32[]{:S(2)}) copy-start(bf16[8,128,576]{1,2,0:T(8,128)(2,1)} %param.21) | copy-start | bytes 3538948
  10.6 15.2 %copy-start.3 = (bf16[8,2048]{1,0:T(8,128)(2,1)S(1)}, bf16[8,2048]{1,0:T(8,128)(2,1)}, u32[]{:S(2)}) copy-start(bf16[8,2048]{1,0:T(8,128)(2,1)} %param.16) | copy-start | bytes 98308
  14.4 47.0 %all-to-all-start.1 = ((bf16[8,2,288]{2,1,0:T(2,128)(2,1)}), bf16[8,2,288]{2,1,0:T(2,128)(2,1)S(1)}, u32[]{:S(2)}, u32[]{:S(2)}) async-start(bf16[8,2,288]{2,1,0:T(2,128)(2,1)} %reshape.210), calls=%async_computation.1 | async-start | bytes 24576 | tf_op jit(solution)/shard_map/all_to_all | solution.py:154
  61.3 20.4 %copy-start.7 = (bf16[2048]{0:T(1024)(128)(2,1)S(1)}, bf16[2048]{0:T(1024)(128)(2,1)}, u32[]{:S(2)}) copy-start(bf16[2048]{0:T(1024)(128)(2,1)} %param.26) | copy-start | bytes 12292
  61.4 20.4 %copy-start.8 = (s32[4,2]{0,1:T(2,128)S(1)}, s32[4,2]{0,1:T(2,128)}, u32[]{:S(2)}) copy-start(s32[4,2]{0,1:T(2,128)} %param.28) | copy-start | bytes 100
  61.4 20.4 %copy-start.9 = (s32[32]{0:T(128)S(1)}, s32[32]{0:T(128)}, u32[]{:S(2)}) copy-start(s32[32]{0:T(128)} %param.29) | copy-start | bytes 388
  61.4 17.1 %all-to-all-start = ((bf16[8,1,64,576]{3,2,1,0:T(8,128)(2,1)}), bf16[8,1,64,576]{3,2,1,0:T(8,128)(2,1)S(1)}, u32[]{:S(2)}, u32[]{:S(2)}) async-start(bf16[8,1,64,576]{3,2,1,0:T(8,128)(2,1)} %copy.91), calls=%async_computation | async-start | bytes 1310720 | tf_op jit(solution)/shard_map/all_to_all | solution.py:153
  66.8 76.7 %all-gather.6.cloned.1.call-start = ((), (), s32[]{:S(2)}) async-start(), calls=%async_computation.2 | async-start | bytes 2359296 | tf_op jit(solution)/shard_map/all_gather | solution.py:22
  67.6 77.0 %copy-start.4 = (bf16[4,576]{1,0:T(4,128)(2,1)}, bf16[4,576]{1,0:T(4,128)(2,1)S(1)}, u32[]{:S(2)}) copy-start(bf16[4,576]{1,0:T(4,128)(2,1)S(1)} %broadcast_select_fusion.7) | copy-start | bytes 13828
  79.2 65.3 %copy-start.2 = (bf16[4,64,576]{2,1,0:T(8,128)(2,1)}, bf16[4,64,576]{2,1,0:T(8,128)(2,1)S(1)}, u32[]{:S(2)}) copy-start(bf16[4,64,576]{2,1,0:T(8,128)(2,1)S(1)} %broadcast_select_fusion) | copy-start | bytes 884740
  155.7 47.7 %copy-start.5 = (bf16[8,256]{1,0:T(8,128)(2,1)}, bf16[8,256]{1,0:T(8,128)(2,1)S(1)}, u32[]{:S(2)}) copy-start(bf16[8,256]{1,0:T(8,128)(2,1)S(1)} %fusion.10) | copy-start | bytes 12292
Sparse Core Ops, SparseCore 0:
  81.9 48.8 all-gather.5
where the time goes:
time: 250 us; the launch traced here: 248 us
  blocking collectives  169 us (68%)
  matrix products  19.7 us (8%)
  local copies, waits for them, and re-layouts  15.7 us (6%)
  between operations  14.4 us (6%)
  starting transfers between devices  12.7 us (5%)
  waiting for transfers between devices  10.5 us (4%)
  other arithmetic  5.91 us (2%)
    all_gather x2, blocking collectives, merged(): everything = jax.tree.map(lambda part: lax.all_gather(part, axis), x)  61.2 us
    all_gather x1, blocking collectives, body(): lax.all_gather(hidden_out[None], ('seq', 'mp'), axis=0, tiled=True)  40 us
    pmax x1, blocking collectives, body(): best_all = lax.pmax(local_best, ('seq', 'mp'))  36.8 us
    all_gather x1, blocking collectives, body(): lax.all_gather(query_part, 'seq', axis=1, tiled=True)  31.2 us
    all_to_all x1, waiting for transfers between devices, body(): lax.all_to_all(send_rows, 'seq', split_axis=0, concat_axis=0, tiled=True)  10.5 us
    all_to_all x1, starting transfers between devices, body(): lax.all_to_all(send_summary, 'seq', split_axis=0, concat_axis=0, tiled=True)  7.25 us
    dot_general x1, matrix products, body(): logits = jnp.dot(normed, head_weight, preferred_element_type=jnp.float32)  7.24 us
    dynamic_slice x7, local copies, waits for them, and re-layouts, step(): return combine(so_far, jax.tree.map(lambda part: part[k], everything))  6.83 us
  transfers between devices with their start and end apart: 3, of which 1 were waited for; matrix products, arithmetic and copies ran while one was open for 4% of the time, Pallas kernels for 0%

commit v1 on v0

--- a/solution.py
+++ b/solution.py
@@ -1,6 +1,10 @@
+import functools
+
 import jax
 import jax.numpy as jnp
 from jax import lax
+from jax.experimental import pallas as pl
+from jax.experimental.pallas import tpu as pltpu
 from jax.sharding import PartitionSpec as P
 
 H = 16
@@ -203,6 +207,554 @@
     return (packed_rows, packed_summary, hidden_out, state_norm, top_logit)
 
 
+F32 = jnp.float32
+BF16 = jnp.bfloat16
+PAIR = 2 * RQ
+
+
+def to_peer(src, dst, send_sem, recv_sem, device):
+    copy = pltpu.make_async_remote_copy(
+        src_ref=src,
+        dst_ref=dst,
+        send_sem=send_sem,
+        recv_sem=recv_sem,
+        device_id=device,
+        device_id_type=pl.DeviceIdType.MESH,
+    )
+    copy.start()
+    return copy
+
+
+def as_row(column):
+    wide = jnp.broadcast_to(column[:, :1], (RQ, RQ))
+    sub = lax.broadcasted_iota(jnp.int32, (RQ, RQ), 0)
+    lane = lax.broadcasted_iota(jnp.int32, (RQ, RQ), 1)
+    return jnp.sum(jnp.where(sub == lane, wide, 0.0), axis=0, keepdims=True)
+
+
+def unfold(part):
+    wide = part.astype(F32)
+    return jnp.concatenate([wide[:RQ], wide[RQ:]], axis=1)
+
+
+def fold(x):
+    width = x.shape[1] // 2
+    return jnp.concatenate([x[:, :width], x[:, width:]], axis=0)
+
+
+def layer_kernel(
+    seq_count,
+    mp_count,
+    vocab_width,
+    tile,
+    hidden_ref,
+    keep_ref,
+    drop_ref,
+    gain_ref,
+    dest_ref,
+    ranges_ref,
+    ids_ref,
+    query_hbm,
+    absorb_hbm,
+    up_hbm,
+    out_hbm,
+    cache_hbm,
+    head_hbm,
+    rows_out,
+    summary_out,
+    hidden_out,
+    norm_out,
+    top_out,
+    query_w,
+    absorb_w,
+    up_w,
+    out_w,
+    cache,
+    head_w,
+    query_recv,
+    query_flat,
+    kept,
+    summ,
+    rows_send,
+    rows_recv,
+    summ_send,
+    summ_recv,
+    part_send,
+    part_recv,
+    value_recv,
+    hidden_all,
+    mp_best,
+    mp_best_recv,
+    seq_best,
+    local_sem,
+    q_send,
+    q_recv,
+    r_send,
+    r_recv,
+    s_send,
+    s_recv,
+    p_send,
+    p_recv,
+    v_send,
+    v_recv,
+    h_send,
+    h_recv,
+    g_send,
+    g_recv,
+    a_send,
+    a_recv,
+    b_send,
+    b_recv,
+):
+    me = lax.axis_index("seq")
+    my_mp = lax.axis_index("mp")
+    slot_count = RQ // 2
+    block_count = dest_ref.shape[1]
+    row_width = LAT + ROPE
+    head_width = NOPE + ROPE
+
+    def seq_peer(k):
+        return lax.rem(me + k, seq_count)
+
+    def mp_peer(k):
+        return lax.rem(my_mp + k, mp_count)
+
+    def load(i, src, dst):
+        copy = pltpu.make_async_copy(src, dst, local_sem.at[i])
+        copy.start()
+        return copy
+
+    query_load = load(0, query_hbm, query_w)
+    cache_load = load(1, cache_hbm, cache)
+    absorb_load = load(2, absorb_hbm, absorb_w)
+
+    barrier = pltpu.get_barrier_semaphore()
+    for k in range(1, seq_count):
+        pl.semaphore_signal(
+            barrier, inc=1, device_id=(seq_peer(k), my_mp), device_id_type=pl.DeviceIdType.MESH
+        )
+    for k in range(1, mp_count):
+        pl.semaphore_signal(
+            barrier, inc=1, device_id=(me, mp_peer(k)), device_id_type=pl.DeviceIdType.MESH
+        )
+
+    keep = jnp.concatenate([keep_ref[:, 0, :], keep_ref[:, 0, :]], axis=1).astype(F32)
+    keep_t = jnp.transpose(keep)[:KB]
+    position = lax.broadcasted_iota(jnp.int32, (KB, BLK), 1).astype(F32)
+    request_sub = lax.broadcasted_iota(jnp.int32, (RQ, BLK), 0)
+    picks = []
+    kept_flag = jnp.zeros((RQ, BLK), F32)
+    for r in range(RQ):
+        pick = jnp.where(jnp.broadcast_to(keep_t[:, r : r + 1], (KB, BLK)) == position, 1.0, 0.0)
+        flag = jnp.sum(pick, axis=0, keepdims=True)
+        kept_flag = jnp.where(request_sub == r, jnp.broadcast_to(flag, (RQ, BLK)), kept_flag)
+        picks.append(pick.astype(BF16))
+    dropped = drop_ref[...].astype(F32) * (1.0 - kept_flag)
+    mass = jnp.sum(dropped, axis=1, keepdims=True)
+
+    query_load.wait()
+    query = jnp.dot(hidden_ref[...], query_w[...], preferred_element_type=F32)
+    query_recv[me] = fold(query).astype(BF16)
+    pl.semaphore_wait(barrier, seq_count + mp_count - 2)
+    sends = []
+    query_copies = [
+        to_peer(
+            query_recv.at[me],
+            query_recv.at[me],
+            q_send.at[k - 1],
+            q_recv.at[k - 1],
+            (seq_peer(k), my_mp),
+        )
+        for k in range(1, seq_count)
+    ]
+    out_load = load(3, out_hbm, out_w)
+    up_load = load(4, up_hbm.at[pl.ds(me * 2, 2)], up_w)
+    head_load = load(5, head_hbm, head_w)
+
+    cache_load.wait()
+    summed = jnp.zeros((PAIR, row_width), F32)
+    pad = jnp.zeros((PAIR - RQ, BLK), F32)
+    for r in range(RQ):
+        kept[r] = jnp.dot(picks[r], cache[r], preferred_element_type=F32).astype(BF16)
+        own = jnp.where(request_sub == r, dropped, 0.0)
+        own = jnp.concatenate([own, pad], axis=0).astype(BF16)
+        summed = summed + jnp.dot(own, cache[r], preferred_element_type=F32)
+    mass_pair = jnp.concatenate([mass, jnp.ones_like(mass)], axis=0)
+    summary = (summed / mass_pair).astype(BF16)
+    summ[...] = summary
+    summary_f = summary.astype(F32)[:RQ]
+    low_part = summary_f[:, :384]
+    high_part = jnp.concatenate([summary_f[:, 384:], jnp.zeros((RQ, 768 - row_width), F32)], axis=1)
+    folded_summary = jnp.concatenate([low_part, high_part], axis=0).astype(BF16)
+    summ_send[...] = folded_summary
+    summ_recv[me] = folded_summary
+
+    owners = [dest_ref[r, me] >> 2 for r in range(RQ)]
+
+    def request_for(owner):
+        chosen = jnp.int32(0)
+        for r in range(RQ):
+            chosen = jnp.where(owners[r] == owner, jnp.int32(r), chosen)
+        return chosen
+
+    rows_recv[me] = kept[request_for(me)]
+    for k in range(1, seq_count):
+        rows_send[k - 1] = kept[request_for(seq_peer(k))]
+
+    def start_pack():
+        started = []
+        for k in range(1, seq_count):
+            started.append(
+                to_peer(
+                    summ_send,
+                    summ_recv.at[me],
+                    s_send.at[k - 1],
+                    s_recv.at[k - 1],
+                    (seq_peer(k), my_mp),
+                )
+            )
+            started.append(
+                to_peer(
+                    rows_send.at[k - 1],
+                    rows_recv.at[me],
+                    r_send.at[k - 1],
+                    r_recv.at[k - 1],
+                    (seq_peer(k), my_mp),
+                )
+            )
+        return started
+
+    pack_copies = start_pack()
+
+    absorb_load.wait()
+    for copy in query_copies:
+        copy.wait_recv()
+    first_half = lax.broadcasted_iota(jnp.int32, (PAIR, NOPE), 0) < RQ
+    for s in range(seq_count):
+        part = query_recv[s]
+        nope = part[:, :NOPE].astype(F32)
+        split = jnp.concatenate(
+            [jnp.where(first_half, nope, 0.0), jnp.where(first_half, 0.0, nope)], axis=1
+        ).astype(BF16)
+        weight = absorb_w[2 * s : 2 * s + 2].reshape(2 * NOPE, LAT)
+        latent = jnp.dot(split, weight, preferred_element_type=F32).astype(BF16)
+        query_flat[PAIR * s : PAIR * (s + 1), :LAT] = latent
+        query_flat[PAIR * s : PAIR * (s + 1), LAT:] = part[:, NOPE:]
+
+    rows = H * RQ
+    score_scale = (NOPE + ROPE) ** (-0.5)
+    contract = (((1,), (1,)), ((), ()))
+    flat = query_flat[...]
+    kept_all = kept[...].reshape(RQ * KB, row_width)
+    row_scores = lax.dot_general(flat, kept_all, contract, preferred_element_type=F32)
+    summ_scores = lax.dot_general(flat, summ[...], contract, preferred_element_type=F32)
+    row_request = lax.broadcasted_iota(jnp.int32, (rows, RQ * KB), 0) & (RQ - 1)
+    col_request = lax.broadcasted_iota(jnp.int32, (rows, RQ * KB), 1) // KB
+    row_scores = jnp.where(row_request == col_request, row_scores * score_scale, NEGATIVE)
+    summ_request = lax.broadcasted_iota(jnp.int32, (rows, PAIR), 0) & (RQ - 1)
+    summ_column = lax.broadcasted_iota(jnp.int32, (rows, PAIR), 1)
+    summ_scores = summ_scores * score_scale + jnp.log(F32(BLK - KB))
+    summ_scores = jnp.where(summ_request == summ_column, summ_scores, NEGATIVE)
+    maxima = jnp.maximum(
+        jnp.max(row_scores, axis=1, keepdims=True), jnp.max(summ_scores, axis=1, keepdims=True)
+    )
+    row_weights = jnp.exp(row_scores - maxima)
+    summ_weights = jnp.exp(summ_scores - maxima)
+    totals = jnp.sum(row_weights, axis=1, keepdims=True) + jnp.sum(
+        summ_weights, axis=1, keepdims=True
+    )
+    weighted = jnp.dot(
+        row_weights.astype(BF16), kept_all[:, :LAT], preferred_element_type=F32
+    ) + jnp.dot(summ_weights.astype(BF16), summ[:, :LAT], preferred_element_type=F32)
+    live_rows = lax.broadcasted_iota(jnp.int32, (rows, 128), 0) & (RQ - 1)
+    level = jnp.broadcast_to(maxima + jnp.log(totals), (rows, 128))
+    for r in range(RQ):
+        level = jnp.where((live_rows == r) & (owners[r] < 0), NEGATIVE, level)
+    high = level.astype(BF16).astype(F32)
+    middle = (level - high).astype(BF16).astype(F32)
+    low = level - high - middle
+    lane = lax.broadcasted_iota(jnp.int32, (rows, 128), 1)
+    terms = jnp.where(
+        lane == 0, high, jnp.where(lane == 1, middle, jnp.where(lane == 2, low, 0.0))
+    )
+    part_send[:, :, :LAT] = (weighted / totals).astype(BF16).reshape(seq_count, PAIR, LAT)
+    part_send[:, :, LAT:] = terms.astype(BF16).reshape(seq_count, PAIR, 128)
+    part_copies = [
+        to_peer(
+            part_send.at[seq_peer(k)],
+            part_recv.at[me],
+            p_send.at[k - 1],
+            p_recv.at[k - 1],
+            (seq_peer(k), my_mp),
+        )
+        for k in range(1, seq_count)
+    ]
+    part_recv[me] = part_send[me]
+
+    total_rows = mp_count * RQ
+    window_row = lax.broadcasted_iota(jnp.int32, (total_rows, 128), 0)
+    window_low = jnp.zeros((total_rows, 128), jnp.int32)
+    window_high = jnp.zeros((total_rows, 128), jnp.int32)
+    for row in range(total_rows):
+        tenant = ids_ref[row]
+        window_low = jnp.where(window_row == row, ranges_ref[tenant, 0], window_low)
+        window_high = jnp.where(window_row == row, ranges_ref[tenant, 1], window_high)
+    vocab_start = (me * mp_count + my_mp) * vocab_width
+    window_low = window_low - vocab_start
+    window_high = window_high - vocab_start
+
+    slot_code = [jnp.int32(0)] * slot_count
+    for r in range(RQ):
+        for b in range(block_count):
+            offset = dest_ref[r, b] - me * slot_count
+            for j in range(slot_count):
+                slot_code[j] = jnp.where(offset == j, jnp.int32(b * RQ + r), slot_code[j])
+
+    up_load.wait()
+    for copy in part_copies:
+        copy.wait_recv()
+    levels = [
+        jnp.sum(part_recv[s, :, LAT:].astype(F32), axis=1, keepdims=True)
+        for s in range(seq_count)
+    ]
+    peak = functools.reduce(jnp.maximum, levels)
+    factors = [jnp.exp(part_level - peak) for part_level in levels]
+    merged_sum = functools.reduce(
+        jnp.add, [factors[s] * part_recv[s, :, :LAT].astype(F32) for s in range(seq_count)]
+    )
+    attended = (merged_sum / functools.reduce(jnp.add, factors)).astype(BF16).astype(F32)
+    first_wide = lax.broadcasted_iota(jnp.int32, (PAIR, LAT), 0) < RQ
+    split = jnp.concatenate(
+        [jnp.where(first_wide, attended, 0.0), jnp.where(first_wide, 0.0, attended)], axis=1
+    ).astype(BF16)
+    values = jnp.dot(split, up_w[...].reshape(2 * LAT, VH), preferred_element_type=F32)
+    value_recv[me] = values.astype(BF16)
+    value_copies = [
+        to_peer(
+            value_recv.at[me],
+            value_recv.at[me],
+            v_send.at[k - 1],
+            v_recv.at[k - 1],
+            (seq_peer(k), my_mp),
+        )
+        for k in range(1, seq_count)
+    ]
+    out_load.wait()
+    for copy in value_copies:
+        copy.wait_recv()
+    all_values = jnp.concatenate(
+        [unfold(value_recv[s]) for s in range(seq_count)], axis=1
+    ).astype(BF16)
+    col_width = out_w.shape[1]
+    residual = hidden_ref[:, pl.ds(pl.multiple_of(me * col_width, 128), col_width)]
+    hidden = residual.astype(F32) + jnp.dot(all_values, out_w[...], preferred_element_type=F32)
+    hidden = hidden.astype(BF16)
+    hidden_out[...] = hidden
+    hidden_all[my_mp, me] = fold(hidden.astype(F32)).astype(BF16)
+
+    hidden_copies = [
+        to_peer(
+            hidden_all.at[my_mp, me],
+            hidden_all.at[my_mp, me],
+            h_send.at[k - 1],
+            h_recv.at[k - 1],
+            (seq_peer(k), my_mp),
+        )
+        for k in range(1, seq_count)
+    ]
+    for copy in hidden_copies:
+        copy.wait_recv()
+    group_copies = [
+        to_peer(
+            hidden_all.at[my_mp],
+            hidden_all.at[my_mp],
+            g_send.at[k - 1],
+            g_recv.at[k - 1],
+            (me, mp_peer(k)),
+        )
+        for k in range(1, mp_count)
+    ]
+    own_rows = jnp.concatenate(
+        [unfold(hidden_all[my_mp, s]) for s in range(seq_count)], axis=1
+    )
+    own_norm = jnp.sqrt(jnp.mean(own_rows * own_rows, axis=1, keepdims=True))
+    norm_out[...] = as_row(own_norm)
+    gain = gain_ref[...].astype(F32)
+    for copy in group_copies:
+        copy.wait_recv()
+    normed = []
+    for m in range(mp_count):
+        group = jnp.concatenate([unfold(hidden_all[m, s]) for s in range(seq_count)], axis=1)
+        mean_sq = jnp.mean(group * group, axis=1, keepdims=True)
+        normed.append(group * lax.rsqrt(mean_sq + 1e-06) * gain)
+    normed = jnp.concatenate(normed, axis=0).astype(BF16)
+
+    head_load.wait()
+    lane = lax.broadcasted_iota(jnp.int32, (total_rows, 128), 1)
+
+    def head_step(n, best):
+        start = pl.multiple_of(n * tile, 128)
+        logits = jnp.dot(normed, head_w[:, pl.ds(start, tile)], preferred_element_type=F32)
+        for i in range(tile // 128):
+            column = lane + (start + i * 128)
+            allowed = (column >= window_low) & (column < window_high)
+            best = jnp.maximum(
+                best, jnp.where(allowed, logits[:, i * 128 : (i + 1) * 128], NEGATIVE)
+            )
+        return best
+
+    best = lax.fori_loop(
+        0, vocab_width // tile, head_step, jnp.full((total_rows, 128), NEGATIVE, F32)
+    )
+    best = jnp.broadcast_to(jnp.max(best, axis=1, keepdims=True), (total_rows, 128))
+    mp_best[...] = best.reshape(mp_count, RQ, 128)
+    mp_best_recv[my_mp] = mp_best[my_mp]
+    best_copies = [
+        to_peer(
+            mp_best.at[mp_peer(k)],
+            mp_best_recv.at[my_mp],
+            a_send.at[k - 1],
+            a_recv.at[k - 1],
+            (me, mp_peer(k)),
+        )
+        for k in range(1, mp_count)
+    ]
+    for copy in best_copies:
+        copy.wait_recv()
+    seq_best[me] = jnp.max(mp_best_recv[...], axis=0)
+    last_copies = [
+        to_peer(
+            seq_best.at[me],
+            seq_best.at[me],
+            b_send.at[k - 1],
+            b_recv.at[k - 1],
+            (seq_peer(k), my_mp),
+        )
+        for k in range(1, seq_count)
+    ]
+
+    for copy in pack_copies:
+        copy.wait_recv()
+    half_sub = lax.broadcasted_iota(jnp.int32, (PAIR, 384), 0)
+    for j in range(slot_count):
+        source = slot_code[j] // RQ
+        request = slot_code[j] % RQ
+        rows_out[j] = rows_recv[source]
+        both = summ_recv[source].astype(F32)
+        low_row = jnp.sum(jnp.where(half_sub == request, both, 0.0), axis=0, keepdims=True)
+        high_row = jnp.sum(jnp.where(half_sub == request + RQ, both, 0.0), axis=0, keepdims=True)
+        line = jnp.concatenate([low_row, high_row[:, : row_width - 384]], axis=1)
+        summary_out[j : j + 1, :] = line
+
+    for copy in last_copies:
+        copy.wait_recv()
+    top_out[...] = as_row(jnp.max(seq_best[...], axis=0))
+    for copy in (
+        query_copies
+        + pack_copies
+        + part_copies
+        + value_copies
+        + hidden_copies
+        + group_copies
+        + best_copies
+        + last_copies
+    ):
+        copy.wait_send()
+
+
+def fused_body(
+    hidden_in,
+    query_weight,
+    key_absorb,
+    value_up,
+    out_weight,
+    latent_cache,
+    cache_lengths,
+    keep_lists,
+    drop_weights,
+    pack_dest,
+    final_gain,
+    head_weight,
+    tenant_ranges,
+    tenant_ids,
+):
+    seq_count = lax.axis_size("seq")
+    mp_count = lax.axis_size("mp")
+    row_width = LAT + ROPE
+    slot_count = RQ // 2
+    depth, vocab_width = head_weight.shape
+    tile = next(t for t in (640, 512, 384, 256, 128) if vocab_width % t == 0)
+    vmem = pl.BlockSpec(memory_space=pltpu.VMEM)
+    smem = pl.BlockSpec(memory_space=pltpu.SMEM)
+    hbm = pl.BlockSpec(memory_space=pl.ANY)
+    seq_sems = pltpu.SemaphoreType.DMA((seq_count - 1,))
+    mp_sems = pltpu.SemaphoreType.DMA((mp_count - 1,))
+    outs = pl.pallas_call(
+        functools.partial(layer_kernel, seq_count, mp_count, vocab_width, tile),
+        out_shape=(
+            jax.ShapeDtypeStruct((slot_count, KB, row_width), BF16),
+            jax.ShapeDtypeStruct((slot_count, row_width), F32),
+            jax.ShapeDtypeStruct((RQ, out_weight.shape[1]), BF16),
+            jax.ShapeDtypeStruct((1, RQ), F32),
+            jax.ShapeDtypeStruct((1, RQ), F32),
+        ),
+        in_specs=[vmem] * 4 + [smem] * 3 + [hbm] * 6,
+        out_specs=(vmem,) * 5,
+        scratch_shapes=[
+            pltpu.VMEM(query_weight.shape, BF16),
+            pltpu.VMEM(key_absorb.shape, BF16),
+            pltpu.VMEM((2,) + value_up.shape[1:], BF16),
+            pltpu.VMEM(out_weight.shape, BF16),
+            pltpu.VMEM(latent_cache.shape, BF16),
+            pltpu.VMEM(head_weight.shape, BF16),
+            pltpu.VMEM((seq_count, PAIR, NOPE + ROPE), BF16),
+            pltpu.VMEM((H * RQ, row_width), BF16),
+            pltpu.VMEM((RQ, KB, row_width), BF16),
+            pltpu.VMEM((PAIR, row_width), BF16),
+            pltpu.VMEM((seq_count - 1, KB, row_width), BF16),
+            pltpu.VMEM((seq_count, KB, row_width), BF16),
+            pltpu.VMEM((PAIR, 384), BF16),
+            pltpu.VMEM((seq_count, PAIR, 384), BF16),
+            pltpu.VMEM((seq_count, PAIR, LAT + 128), BF16),
+            pltpu.VMEM((seq_count, PAIR, LAT + 128), BF16),
+            pltpu.VMEM((seq_count, PAIR, VH), BF16),
+            pltpu.VMEM((mp_count, seq_count, PAIR, out_weight.shape[1] // 2), BF16),
+            pltpu.VMEM((mp_count, RQ, 128), F32),
+            pltpu.VMEM((mp_count, RQ, 128), F32),
+            pltpu.VMEM((seq_count, RQ, 128), F32),
+            pltpu.SemaphoreType.DMA((6,)),
+        ]
+        + [seq_sems] * 12
+        + [mp_sems] * 4
+        + [seq_sems] * 2,
+        compiler_params=pltpu.CompilerParams(
+            collective_id=0, has_side_effects=True, vmem_limit_bytes=48 * 2**20
+        ),
+    )(
+        hidden_in,
+        keep_lists,
+        drop_weights,
+        final_gain.reshape(1, -1),
+        pack_dest,
+        tenant_ranges,
+        tenant_ids,
+        query_weight,
+        key_absorb,
+        value_up,
+        out_weight,
+        latent_cache,
+        head_weight,
+    )
+    packed_rows, packed_summary, hidden_out, state_norm, top_logit = outs
+    return (
+        packed_rows,
+        packed_summary.astype(BF16),
+        hidden_out,
+        state_norm.reshape(RQ),
+        top_logit.reshape(RQ),
+    )
+
+
 def solution(mesh):
     in_specs = (
         P("mp", None),
@@ -227,4 +779,6 @@
         P("mp"),
         P("mp"),
     )
-    return jax.shard_map(body, mesh=mesh, in_specs=in_specs, out_specs=out_specs, check_vma=False)
+    seq_count = mesh.shape["seq"]
+    fused = seq_count * 2 == H
+    return jax.shard_map(fused_body if fused else body, mesh=mesh, in_specs=in_specs, out_specs=out_specs, check_vma=False)

time: 250 us -> 60.9 us (0.24)
  blocking collectives: 169 us -> 0 us
  Pallas kernels: 0 us -> 52.5 us
  matrix products: 19.7 us -> 0 us
  between operations: 14.4 us -> 0.76 us
  starting transfers between devices: 12.7 us -> 0 us
  waiting for transfers between devices: 10.5 us -> 0 us
  local copies, waits for them, and re-layouts: 15.7 us -> 6.84 us
  other arithmetic: 5.91 us -> 0.6 us
    all_gather x4 -> x0, blocking collectives: 132 us -> none  [the longest x2 61.2 us: merged(): everything = jax.tree.map(lambda part: lax.all_gather(part, axis), x)]
    pallas_call x0 -> x1, Pallas kernels: none -> 52.5 us  [fused_body(): pl.pallas_call(functools.partial(layer_kernel, seq_count, mp_count, vocab...]
    pmax x1 -> x0, blocking collectives: 36.8 us -> none  [body(): best_all = lax.pmax(local_best, ('seq', 'mp'))]
    dot_general x14 -> x0, matrix products: 19.7 us -> none  [the longest x1 7.24 us: body(): logits = jnp.dot(normed, head_weight, preferred_element_type=jnp.float32)]
    all_to_all x2 -> x0, starting transfers between devices: 12.6 us -> none  [the longest x1 7.25 us: body(): lax.all_to_all(send_summary, 'seq', split_axis=0, concat_axis=0, tiled=True)]
    all_to_all x2 -> x0, waiting for transfers between devices: 10.5 us -> none  [the longest x1 10.5 us: body(): lax.all_to_all(send_rows, 'seq', split_axis=0, concat_axis=0, tiled=True)]
    dynamic_slice x10 -> x0, local copies, waits for them, and re-layouts: 9.03 us -> none  [the longest x7 6.83 us: step(): return combine(so_far, jax.tree.map(lambda part: part[k], everything))]
    unnamed x25 -> x20, local copies, waits for them, and re-layouts: 1.02 us -> 6.15 us
  transfers between devices with their start and end apart: 3 -> 0, of which waited for: 1 -> 0; matrix products, arithmetic and copies ran while one was open for 4% -> 0% of each run, Pallas kernels for 0% -> 0%
where the time goes in v1:
time: 60.9 us; the launch traced here: 60.7 us
  Pallas kernels  52.5 us (86%)
  local copies, waits for them, and re-layouts  6.84 us (11%)
  between operations  0.76 us (1%)
    pallas_call x1, Pallas kernels, fused_body(): pl.pallas_call(functools.partial(layer_kernel, seq_count, mp_count, vocab...  52.5 us
    unnamed x20, local copies, waits for them, and re-layouts  6.15 us

profile of v1, /device:TPU:0, one launch (start us, length us, event | category | flops | bytes accessed | tf_op | source)
XLA Modules:
  0.0 60.7 jit_solution(17436164576790114879)
XLA Ops:
  0.6 0.0 copy-start.6
  0.6 0.0 copy-start.5
  0.7 0.0 copy-start.4
  0.7 0.0 copy-start.3
  0.7 0.0 copy-start
  0.7 0.0 copy-start.2
  0.7 0.9 %copy.18.ranges_ref = s32[4,2]{1,0:T(4,128)S(1)} copy(s32[4,2]{0,1:T(2,128)} %param.25) | data formatting | bytes 64 | tf_op args[12]
  1.6 0.7 %reshape.19.gain_ref = bf16[1,2048]{1,0:T(2,128)(2,1)S(1)} reshape(bf16[2048]{0:T(1024)(128)(2,1)} %param.23) | data formatting | bytes 8192 | tf_op jit(solution)/shard_map/reshape | solution.py:737
  2.3 1.7 %copy.19.cache_hbm = bf16[8,128,576]{2,1,0:T(8,128)(2,1)S(1)} copy(bf16[8,128,576]{1,2,0:T(8,128)(2,1)} %param.19) | data formatting | bytes 2359296 | tf_op args[5]
  4.0 0.0 copy-done.6
  4.0 0.0 copy-done.5
  4.0 0.0 copy-done.4
  4.0 0.0 copy-done.3
  4.0 0.0 copy-done
  4.0 0.0 copy-done.2
  4.0 0.0 copy-start.1
  4.0 1.2 %copy-done.1 = bf16[2048,256]{1,0:T(8,128)(2,1)S(1)} copy-done((bf16[2048,256]{1,0:T(8,128)(2,1)S(1)}, bf16[2048,256]{1,0:T(8,128)(2,1)}, u32[]{:S(2)}) %copy-start.1) | copy-done | bytes 1048600
  5.2 52.5 %shard_map.164 = (bf16[4,64,576]{2,1,0:T(8,128)(2,1)S(1)}, f32[4,576]{1,0:T(4,128)S(1)}, bf16[8,256]{1,0:T(8,128)(2,1)S(1)}, f32[1,8]{1,0:T(1,128)S(1)}, f32[1,8]{1,0:T(1,128)S(1)}) custom-call(bf16[8,2048]{1,0:T(8,128)(2,1)S(1)} %copy-done.2, s32[8,1,64]{2,1,0:T(1,128)S(1)} %copy-done.3, s32[8,128]{1,0:T(8,128)S(1)} %copy-done.4, ...), custom_call_target="tpu_custom_call" | custom-call | tf_op jit(solution)/shard_map/pallas_call | solution.py:692
  57.8 0.6 convert_element_type.3
  58.4 0.7 %copy.24 = bf16[4,64,576]{2,1,0:T(8,128)(2,1)} copy(bf16[4,64,576]{2,1,0:T(8,128)(2,1)S(1)} %get-tuple-element.20) | data formatting | bytes 589824
  59.1 0.6 copy.25
  59.7 0.5 copy.26
  60.2 0.5 copy.27
Async XLA Ops:
  0.6 3.3 %copy-start.6 = (s32[32]{0:T(128)S(1)}, s32[32]{0:T(128)}, u32[]{:S(2)}) copy-start(s32[32]{0:T(128)} %ids_ref.1) | copy-start | bytes 388
  0.6 3.3 %copy-start.5 = (s32[8,8]{1,0:T(8,128)S(1)}, s32[8,8]{1,0:T(8,128)}, u32[]{:S(2)}) copy-start(s32[8,8]{1,0:T(8,128)} %dest_ref.1) | copy-start | bytes 772
  0.7 3.3 %copy-start.4 = (s32[8,128]{1,0:T(8,128)S(1)}, s32[8,128]{1,0:T(8,128)}, u32[]{:S(2)}) copy-start(s32[8,128]{1,0:T(8,128)} %drop_ref.1) | copy-start | bytes 12292
  0.7 3.3 %copy-start.3 = (s32[8,1,64]{2,1,0:T(1,128)S(1)}, s32[8,1,64]{2,1,0:T(1,128)}, u32[]{:S(2)}) copy-start(s32[8,1,64]{2,1,0:T(1,128)} %keep_ref.1) | copy-start | bytes 6148
  0.7 3.3 %copy-start = (bf16[2048,384]{1,0:T(8,128)(2,1)S(1)}, bf16[2048,384]{1,0:T(8,128)(2,1)}, u32[]{:S(2)}) copy-start(bf16[2048,384]{1,0:T(8,128)(2,1)} %query_hbm.1) | copy-start | bytes 4718596
  0.7 3.3 %copy-start.2 = (bf16[8,2048]{1,0:T(8,128)(2,1)S(1)}, bf16[8,2048]{1,0:T(8,128)(2,1)}, u32[]{:S(2)}) copy-start(bf16[8,2048]{1,0:T(8,128)(2,1)} %hidden_ref.1) | copy-start | bytes 98308
  4.0 1.2 %copy-start.1 = (bf16[2048,256]{1,0:T(8,128)(2,1)S(1)}, bf16[2048,256]{1,0:T(8,128)(2,1)}, u32[]{:S(2)}) copy-start(bf16[2048,256]{1,0:T(8,128)(2,1)} %out_hbm.1) | copy-start | bytes 3145732

commit v2 on v1

--- a/solution.py
+++ b/solution.py
@@ -210,6 +210,10 @@
 F32 = jnp.float32
 BF16 = jnp.bfloat16
 PAIR = 2 * RQ
+LANES = 128
+ROPE_AT = LAT // LANES * KB
+SUMM_AT = ROPE_AT + KB // 2
+MESSAGE = SUMM_AT + PAIR
 
 
 def to_peer(src, dst, send_sem, recv_sem, device):
@@ -275,10 +279,9 @@
     query_flat,
     kept,
     summ,
-    rows_send,
-    rows_recv,
-    summ_send,
-    summ_recv,
+    blocks,
+    block_send,
+    block_recv,
     part_send,
     part_recv,
     value_recv,
@@ -291,8 +294,6 @@
     q_recv,
     r_send,
     r_recv,
-    s_send,
-    s_recv,
     p_send,
     p_recv,
     v_send,
@@ -311,7 +312,7 @@
     slot_count = RQ // 2
     block_count = dest_ref.shape[1]
     row_width = LAT + ROPE
-    head_width = NOPE + ROPE
+    contract = (((1,), (1,)), ((), ()))
 
     def seq_peer(k):
         return lax.rem(me + k, seq_count)
@@ -356,7 +357,6 @@
     query = jnp.dot(hidden_ref[...], query_w[...], preferred_element_type=F32)
     query_recv[me] = fold(query).astype(BF16)
     pl.semaphore_wait(barrier, seq_count + mp_count - 2)
-    sends = []
     query_copies = [
         to_peer(
             query_recv.at[me],
@@ -375,19 +375,31 @@
     summed = jnp.zeros((PAIR, row_width), F32)
     pad = jnp.zeros((PAIR - RQ, BLK), F32)
     for r in range(RQ):
-        kept[r] = jnp.dot(picks[r], cache[r], preferred_element_type=F32).astype(BF16)
+        chosen = lax.dot_general(picks[r], cache[r], contract, preferred_element_type=F32)
+        kept[r] = chosen.astype(BF16)
+        for i in range(LAT // LANES):
+            piece = chosen[:, i * LANES : (i + 1) * LANES]
+            blocks[r, i * KB : (i + 1) * KB, :] = piece.astype(BF16)
+        rope = chosen[:, LAT:]
+        rope = jnp.concatenate([rope[: KB // 2], rope[KB // 2 :]], axis=1)
+        blocks[r, ROPE_AT:SUMM_AT, :] = rope.astype(BF16)
         own = jnp.where(request_sub == r, dropped, 0.0)
         own = jnp.concatenate([own, pad], axis=0).astype(BF16)
-        summed = summed + jnp.dot(own, cache[r], preferred_element_type=F32)
+        summed = summed + lax.dot_general(own, cache[r], contract, preferred_element_type=F32)
     mass_pair = jnp.concatenate([mass, jnp.ones_like(mass)], axis=0)
     summary = (summed / mass_pair).astype(BF16)
     summ[...] = summary
     summary_f = summary.astype(F32)[:RQ]
-    low_part = summary_f[:, :384]
-    high_part = jnp.concatenate([summary_f[:, 384:], jnp.zeros((RQ, 768 - row_width), F32)], axis=1)
-    folded_summary = jnp.concatenate([low_part, high_part], axis=0).astype(BF16)
-    summ_send[...] = folded_summary
-    summ_recv[me] = folded_summary
+    summary_f = jnp.concatenate(
+        [summary_f, jnp.zeros((RQ, 5 * LANES - row_width), F32)], axis=1
+    )
+    line = lax.broadcasted_iota(jnp.int32, (PAIR, LANES), 0)
+    for r in range(RQ):
+        lines = jnp.zeros((PAIR, LANES), F32)
+        for i in range(5):
+            piece = summary_f[r : r + 1, i * LANES : (i + 1) * LANES]
+            lines = jnp.where(line == i, jnp.broadcast_to(piece, (PAIR, LANES)), lines)
+        blocks[r, SUMM_AT:, :] = lines.astype(BF16)
 
     owners = [dest_ref[r, me] >> 2 for r in range(RQ)]
 
@@ -397,34 +409,18 @@
             chosen = jnp.where(owners[r] == owner, jnp.int32(r), chosen)
         return chosen
 
-    rows_recv[me] = kept[request_for(me)]
+    block_recv[me] = blocks[request_for(me)]
     for k in range(1, seq_count):
-        rows_send[k - 1] = kept[request_for(seq_peer(k))]
-
-    def start_pack():
-        started = []
-        for k in range(1, seq_count):
-            started.append(
-                to_peer(
-                    summ_send,
-                    summ_recv.at[me],
-                    s_send.at[k - 1],
-                    s_recv.at[k - 1],
-                    (seq_peer(k), my_mp),
-                )
-            )
-            started.append(
-                to_peer(
-                    rows_send.at[k - 1],
-                    rows_recv.at[me],
-                    r_send.at[k - 1],
-                    r_recv.at[k - 1],
-                    (seq_peer(k), my_mp),
-                )
-            )
-        return started
-
-    pack_copies = start_pack()
+        block_send[k - 1] = blocks[request_for(seq_peer(k))]
+
+    def start_pack(k):
+        return to_peer(
+            block_send.at[k - 1],
+            block_recv.at[me],
+            r_send.at[k - 1],
+            r_recv.at[k - 1],
+            (seq_peer(k), my_mp),
+        )
 
     absorb_load.wait()
     for copy in query_copies:
@@ -443,7 +439,6 @@
 
     rows = H * RQ
     score_scale = (NOPE + ROPE) ** (-0.5)
-    contract = (((1,), (1,)), ((), ()))
     flat = query_flat[...]
     kept_all = kept[...].reshape(RQ * KB, row_width)
     row_scores = lax.dot_general(flat, kept_all, contract, preferred_element_type=F32)
@@ -497,22 +492,23 @@
     window_high = jnp.zeros((total_rows, 128), jnp.int32)
     for row in range(total_rows):
         tenant = ids_ref[row]
-        window_low = jnp.where(window_row == row, ranges_ref[tenant, 0], window_low)
-        window_high = jnp.where(window_row == row, ranges_ref[tenant, 1], window_high)
+        window_low = jnp.where(window_row == row, ranges_ref[0, tenant], window_low)
+        window_high = jnp.where(window_row == row, ranges_ref[1, tenant], window_high)
     vocab_start = (me * mp_count + my_mp) * vocab_width
     window_low = window_low - vocab_start
     window_high = window_high - vocab_start
 
-    slot_code = [jnp.int32(0)] * slot_count
+    slot_source = [jnp.int32(0)] * slot_count
     for r in range(RQ):
         for b in range(block_count):
             offset = dest_ref[r, b] - me * slot_count
             for j in range(slot_count):
-                slot_code[j] = jnp.where(offset == j, jnp.int32(b * RQ + r), slot_code[j])
+                slot_source[j] = jnp.where(offset == j, jnp.int32(b), slot_source[j])
 
     up_load.wait()
     for copy in part_copies:
         copy.wait_recv()
+    pack_copies = [start_pack(k) for k in range(1, seq_count)]
     levels = [
         jnp.sum(part_recv[s, :, LAT:].astype(F32), axis=1, keepdims=True)
         for s in range(seq_count)
@@ -579,7 +575,7 @@
     )
     own_norm = jnp.sqrt(jnp.mean(own_rows * own_rows, axis=1, keepdims=True))
     norm_out[...] = as_row(own_norm)
-    gain = gain_ref[...].astype(F32)
+    gain = gain_ref[...].astype(F32).reshape(1, -1)
     for copy in group_copies:
         copy.wait_recv()
     normed = []
@@ -635,16 +631,19 @@
 
     for copy in pack_copies:
         copy.wait_recv()
-    half_sub = lax.broadcasted_iota(jnp.int32, (PAIR, 384), 0)
+    lines = []
     for j in range(slot_count):
-        source = slot_code[j] // RQ
-        request = slot_code[j] % RQ
-        rows_out[j] = rows_recv[source]
-        both = summ_recv[source].astype(F32)
-        low_row = jnp.sum(jnp.where(half_sub == request, both, 0.0), axis=0, keepdims=True)
-        high_row = jnp.sum(jnp.where(half_sub == request + RQ, both, 0.0), axis=0, keepdims=True)
-        line = jnp.concatenate([low_row, high_row[:, : row_width - 384]], axis=1)
-        summary_out[j : j + 1, :] = line
+        source = slot_source[j]
+        block = block_recv[source]
+        for i in range(LAT // LANES):
+            rows_out[j, :, i * LANES : (i + 1) * LANES] = block[i * KB : (i + 1) * KB]
+        rope = block[ROPE_AT:SUMM_AT].astype(F32)
+        rope = jnp.concatenate([rope[:, :ROPE], rope[:, ROPE:]], axis=0)
+        rows_out[j, :, LAT:] = rope.astype(BF16)
+        tail = block[SUMM_AT:].astype(F32)
+        line = jnp.concatenate([tail[i : i + 1] for i in range(5)], axis=1)
+        lines.append(line[:, :row_width])
+    summary_out[...] = jnp.concatenate(lines, axis=0).astype(BF16)
 
     for copy in last_copies:
         copy.wait_recv()
@@ -660,6 +659,18 @@
         + last_copies
     ):
         copy.wait_send()
+
+
+def publish_kernel(*refs):
+    results, places, sem = refs[:5], refs[5:10], refs[10]
+    copies = [
+        pltpu.make_async_copy(result, place, sem.at[i])
+        for i, (result, place) in enumerate(zip(results, places))
+    ]
+    for copy in copies:
+        copy.start()
+    for copy in copies:
+        copy.wait()
 
 
 def fused_body(
@@ -686,14 +697,14 @@
     tile = next(t for t in (640, 512, 384, 256, 128) if vocab_width % t == 0)
     vmem = pl.BlockSpec(memory_space=pltpu.VMEM)
     smem = pl.BlockSpec(memory_space=pltpu.SMEM)
-    hbm = pl.BlockSpec(memory_space=pl.ANY)
+    hbm = pl.BlockSpec(memory_space=pltpu.HBM)
     seq_sems = pltpu.SemaphoreType.DMA((seq_count - 1,))
     mp_sems = pltpu.SemaphoreType.DMA((mp_count - 1,))
     outs = pl.pallas_call(
         functools.partial(layer_kernel, seq_count, mp_count, vocab_width, tile),
         out_shape=(
             jax.ShapeDtypeStruct((slot_count, KB, row_width), BF16),
-            jax.ShapeDtypeStruct((slot_count, row_width), F32),
+            jax.ShapeDtypeStruct((slot_count, row_width), BF16),
             jax.ShapeDtypeStruct((RQ, out_weight.shape[1]), BF16),
             jax.ShapeDtypeStruct((1, RQ), F32),
             jax.ShapeDtypeStruct((1, RQ), F32),
@@ -705,16 +716,15 @@
             pltpu.VMEM(key_absorb.shape, BF16),
             pltpu.VMEM((2,) + value_up.shape[1:], BF16),
             pltpu.VMEM(out_weight.shape, BF16),
-            pltpu.VMEM(latent_cache.shape, BF16),
+            pltpu.VMEM((RQ, row_width, BLK), BF16),
             pltpu.VMEM(head_weight.shape, BF16),
             pltpu.VMEM((seq_count, PAIR, NOPE + ROPE), BF16),
             pltpu.VMEM((H * RQ, row_width), BF16),
             pltpu.VMEM((RQ, KB, row_width), BF16),
             pltpu.VMEM((PAIR, row_width), BF16),
-            pltpu.VMEM((seq_count - 1, KB, row_width), BF16),
-            pltpu.VMEM((seq_count, KB, row_width), BF16),
-            pltpu.VMEM((PAIR, 384), BF16),
-            pltpu.VMEM((seq_count, PAIR, 384), BF16),
+            pltpu.VMEM((RQ, MESSAGE, LANES), BF16),
+            pltpu.VMEM((seq_count - 1, MESSAGE, LANES), BF16),
+            pltpu.VMEM((seq_count, MESSAGE, LANES), BF16),
             pltpu.VMEM((seq_count, PAIR, LAT + 128), BF16),
             pltpu.VMEM((seq_count, PAIR, LAT + 128), BF16),
             pltpu.VMEM((seq_count, PAIR, VH), BF16),
@@ -724,31 +734,38 @@
             pltpu.VMEM((seq_count, RQ, 128), F32),
             pltpu.SemaphoreType.DMA((6,)),
         ]
-        + [seq_sems] * 12
+        + [seq_sems] * 10
         + [mp_sems] * 4
         + [seq_sems] * 2,
         compiler_params=pltpu.CompilerParams(
-            collective_id=0, has_side_effects=True, vmem_limit_bytes=48 * 2**20
+            collective_id=0, has_side_effects=True, vmem_limit_bytes=213 * 2**18
         ),
     )(
         hidden_in,
         keep_lists,
         drop_weights,
-        final_gain.reshape(1, -1),
+        final_gain,
         pack_dest,
-        tenant_ranges,
+        jnp.swapaxes(tenant_ranges, 0, 1),
         tenant_ids,
         query_weight,
         key_absorb,
         value_up,
         out_weight,
-        latent_cache,
+        jnp.swapaxes(latent_cache, 1, 2),
         head_weight,
     )
+    outs = pl.pallas_call(
+        publish_kernel,
+        out_shape=tuple(jax.ShapeDtypeStruct(out.shape, out.dtype) for out in outs),
+        in_specs=[vmem] * 5,
+        out_specs=(hbm,) * 5,
+        scratch_shapes=[pltpu.SemaphoreType.DMA((5,))],
+    )(*outs)
     packed_rows, packed_summary, hidden_out, state_norm, top_logit = outs
     return (
         packed_rows,
-        packed_summary.astype(BF16),
+        packed_summary,
         hidden_out,
         state_norm.reshape(RQ),
         top_logit.reshape(RQ),

time: 60.9 us -> 59.4 us (0.975)
  Pallas kernels: 52.5 us -> 50.5 us
  local copies, waits for them, and re-layouts: 6.84 us -> 7.79 us
    pallas_call x1, Pallas kernels: 52.5 us -> 48.8 us  [fused_body(): pl.pallas_call(functools.partial(layer_kernel, seq_count, mp_count, vocab...]
    pallas_call x0 -> x1, Pallas kernels: none -> 1.77 us  [fused_body(): pl.pallas_call(publish_kernel, out_shape=tuple((jax.ShapeDtypeStruct(out....]
    unnamed x20 -> x24, local copies, waits for them, and re-layouts: 6.15 us -> 7.79 us
    reshape x1 -> x0, local copies, waits for them, and re-layouts: 0.69 us -> none  [fused_body(): final_gain.reshape(1, -1)]
where the time goes in v2:
time: 59.4 us; the launch traced here: 59 us
  Pallas kernels  50.5 us (85%)
  local copies, waits for them, and re-layouts  7.79 us (13%)
  between operations  0.67 us (1%)
    pallas_call x1, Pallas kernels, fused_body(): pl.pallas_call(functools.partial(layer_kernel, seq_count, mp_count, vocab...  48.8 us
    unnamed x24, local copies, waits for them, and re-layouts  7.79 us
    pallas_call x1, Pallas kernels, fused_body(): pl.pallas_call(publish_kernel, out_shape=tuple((jax.ShapeDtypeStruct(out....  1.77 us

profile of v2, /device:TPU:0, one launch (start us, length us, event | category | flops | bytes accessed | tf_op | source)
XLA Modules:
  0.0 59.0 jit_solution(5855514375263476944)
XLA Ops:
  0.6 0.0 copy-start.1
  0.6 0.7 %copy-done.1 = bf16[8,2048]{1,0:T(8,128)(2,1)S(1)} copy-done((bf16[8,2048]{1,0:T(8,128)(2,1)S(1)}, bf16[8,2048]{1,0:T(8,128)(2,1)}, u32[]{:S(2)}) %copy-start.1) | copy-done | bytes 32792
  1.4 0.0 copy-start.4
  1.4 0.7 %copy-done.4 = s32[8,1,64]{2,1,0:T(1,128)S(1)} copy-done((s32[8,1,64]{2,1,0:T(1,128)S(1)}, s32[8,1,64]{2,1,0:T(1,128)}, u32[]{:S(2)}) %copy-start.4) | copy-done | bytes 2072
  2.1 0.0 copy-start.5
  2.1 0.7 %copy-done.5 = s32[8,128]{1,0:T(8,128)S(1)} copy-done((s32[8,128]{1,0:T(8,128)S(1)}, s32[8,128]{1,0:T(8,128)}, u32[]{:S(2)}) %copy-start.5) | copy-done | bytes 4120
  2.8 0.0 copy-start.6
  2.8 0.7 %copy-done.6 = bf16[2048]{0:T(1024)(128)(2,1)S(1)} copy-done((bf16[2048]{0:T(1024)(128)(2,1)S(1)}, bf16[2048]{0:T(1024)(128)(2,1)}, u32[]{:S(2)}) %copy-start.6) | copy-done | bytes 4120
  3.5 0.0 copy-start.7
  3.5 0.7 %copy-done.7 = s32[8,8]{1,0:T(8,128)S(1)} copy-done((s32[8,8]{1,0:T(8,128)S(1)}, s32[8,8]{1,0:T(8,128)}, u32[]{:S(2)}) %copy-start.7) | copy-done | bytes 280
  4.1 0.7 %copy-done.8 = s32[4,2]{0,1:T(2,128)S(1)} copy-done((s32[4,2]{0,1:T(2,128)S(1)}, s32[4,2]{0,1:T(2,128)}, u32[]{:S(2)}) %copy-start.8) | copy-done | bytes 56
  4.8 0.0 copy-start.9
  4.8 0.7 %copy-done.9 = s32[32]{0:T(128)S(1)} copy-done((s32[32]{0:T(128)S(1)}, s32[32]{0:T(128)}, u32[]{:S(2)}) %copy-start.9) | copy-done | bytes 152
  5.5 48.8 %shard_map.164 = (bf16[4,64,576]{2,1,0:T(8,128)(2,1)S(1)}, bf16[4,576]{1,0:T(4,128)(2,1)S(1)}, bf16[8,256]{1,0:T(8,128)(2,1)S(1)}, f32[1,8]{1,0:T(1,128)S(1)}, f32[1,8]{1,0:T(1,128)S(1)}) custom-call(bf16[8,2048]{1,0:T(8,128)(2,1)S(1)} %copy-done.1, s32[8,1,64]{2,1,0:T(1,128)S(1)} %copy-done.4, s32[8,128]{1,0:T(8,128)S(1)} %copy-done.5, ...), custom_call_target="tpu_custom_call" | custom-call | tf_op jit(solution)/shard_map/pallas_call | solution.py:703
  54.3 0.0 copy-start
  54.3 0.7 %copy-done = bf16[4,64,576]{2,1,0:T(8,128)(2,1)} copy-done((bf16[4,64,576]{2,1,0:T(8,128)(2,1)}, bf16[4,64,576]{2,1,0:T(8,128)(2,1)S(1)}, u32[]{:S(2)}) %copy-start) | copy-done | bytes 294936
  55.0 0.0 copy-start.2
  55.0 0.6 %copy-done.2 = bf16[4,576]{1,0:T(4,128)(2,1)} copy-done((bf16[4,576]{1,0:T(4,128)(2,1)}, bf16[4,576]{1,0:T(4,128)(2,1)S(1)}, u32[]{:S(2)}) %copy-start.2) | copy-done | bytes 4632
  55.6 0.6 copy-done.3
  56.2 0.0 copy-start.10
  56.2 0.5 copy-done.10
  56.7 0.0 copy-start.11
  56.7 0.6 copy-done.11
  57.2 1.8 %shard_map.165 = (bf16[4,64,576]{2,1,0:T(8,128)(2,1)}, bf16[4,576]{1,0:T(4,128)(2,1)}, bf16[8,256]{1,0:T(8,128)(2,1)}, f32[1,8]{1,0:T(1,128)}, f32[1,8]{1,0:T(1,128)}) custom-call(bf16[4,64,576]{2,1,0:T(8,128)(2,1)} %copy-done, bf16[4,576]{1,0:T(4,128)(2,1)} %copy-done.2, bf16[8,256]{1,0:T(8,128)(2,1)} %copy-done.3, f32[1,8]{1,0:T(1,128)} %copy-done.10, ...), custom_call_target="tpu_custom_call" | custom-call | tf_op jit(solution)/shard_map/pallas_call | solution.py:758
  (2 shorter events, 0.0 us)
Async XLA Ops:
  0.6 0.8 %copy-start.1 = (bf16[8,2048]{1,0:T(8,128)(2,1)S(1)}, bf16[8,2048]{1,0:T(8,128)(2,1)}, u32[]{:S(2)}) copy-start(bf16[8,2048]{1,0:T(8,128)(2,1)} %hidden_ref.1) | copy-start | bytes 98308
  1.4 0.7 %copy-start.4 = (s32[8,1,64]{2,1,0:T(1,128)S(1)}, s32[8,1,64]{2,1,0:T(1,128)}, u32[]{:S(2)}) copy-start(s32[8,1,64]{2,1,0:T(1,128)} %keep_ref.1) | copy-start | bytes 6148
  2.1 0.7 %copy-start.5 = (s32[8,128]{1,0:T(8,128)S(1)}, s32[8,128]{1,0:T(8,128)}, u32[]{:S(2)}) copy-start(s32[8,128]{1,0:T(8,128)} %drop_ref.1) | copy-start | bytes 12292
  2.8 0.7 %copy-start.6 = (bf16[2048]{0:T(1024)(128)(2,1)S(1)}, bf16[2048]{0:T(1024)(128)(2,1)}, u32[]{:S(2)}) copy-start(bf16[2048]{0:T(1024)(128)(2,1)} %gain_ref.1) | copy-start | bytes 12292
  3.5 0.7 %copy-start.7 = (s32[8,8]{1,0:T(8,128)S(1)}, s32[8,8]{1,0:T(8,128)}, u32[]{:S(2)}) copy-start(s32[8,8]{1,0:T(8,128)} %dest_ref.1) | copy-start | bytes 772
  4.1 0.7 %copy-start.8 = (s32[4,2]{0,1:T(2,128)S(1)}, s32[4,2]{0,1:T(2,128)}, u32[]{:S(2)}) copy-start(s32[4,2]{0,1:T(2,128)} %param.25) | copy-start | bytes 100
  4.8 0.7 %copy-start.9 = (s32[32]{0:T(128)S(1)}, s32[32]{0:T(128)}, u32[]{:S(2)}) copy-start(s32[32]{0:T(128)} %ids_ref.1) | copy-start | bytes 388
  54.3 0.7 %copy-start = (bf16[4,64,576]{2,1,0:T(8,128)(2,1)}, bf16[4,64,576]{2,1,0:T(8,128)(2,1)S(1)}, u32[]{:S(2)}) copy-start(bf16[4,64,576]{2,1,0:T(8,128)(2,1)S(1)} %get-tuple-element.15.refs_0_) | copy-start | bytes 884740
  55.0 0.6 %copy-start.2 = (bf16[4,576]{1,0:T(4,128)(2,1)}, bf16[4,576]{1,0:T(4,128)(2,1)S(1)}, u32[]{:S(2)}) copy-start(bf16[4,576]{1,0:T(4,128)(2,1)S(1)} %get-tuple-element.16.refs_1_) | copy-start | bytes 13828
  55.6 0.6 copy-start.3
  56.2 0.5 copy-start.10
  56.7 0.6 copy-start.11

commit v3 on v2

--- a/solution.py
+++ b/solution.py
@@ -251,6 +251,24 @@
     mp_count,
     vocab_width,
     tile,
+    hidden_hbm,
+    keep_hbm,
+    drop_hbm,
+    gain_hbm,
+    dest_hbm,
+    ranges_hbm,
+    ids_hbm,
+    query_hbm,
+    absorb_hbm,
+    up_hbm,
+    out_hbm,
+    cache_hbm,
+    head_hbm,
+    rows_hbm,
+    summary_hbm,
+    hidden_out_hbm,
+    norm_hbm,
+    top_hbm,
     hidden_ref,
     keep_ref,
     drop_ref,
@@ -258,12 +276,6 @@
     dest_ref,
     ranges_ref,
     ids_ref,
-    query_hbm,
-    absorb_hbm,
-    up_hbm,
-    out_hbm,
-    cache_hbm,
-    head_hbm,
     rows_out,
     summary_out,
     hidden_out,
@@ -286,10 +298,9 @@
     part_recv,
     value_recv,
     hidden_all,
-    mp_best,
-    mp_best_recv,
-    seq_best,
+    best_all,
     local_sem,
+    store_sem,
     q_send,
     q_recv,
     r_send,
@@ -302,8 +313,6 @@
     h_recv,
     g_send,
     g_recv,
-    a_send,
-    a_recv,
     b_send,
     b_recv,
 ):
@@ -325,19 +334,29 @@
         copy.start()
         return copy
 
-    query_load = load(0, query_hbm, query_w)
-    cache_load = load(1, cache_hbm, cache)
-    absorb_load = load(2, absorb_hbm, absorb_w)
-
+    keep_load = load(0, keep_hbm, keep_ref)
+    drop_load = load(1, drop_hbm, drop_ref)
+    hidden_load = load(2, hidden_hbm, hidden_ref)
+    query_load = load(3, query_hbm, query_w)
+    dest_load = load(4, dest_hbm, dest_ref)
+    cache_load = load(5, cache_hbm, cache)
+    gain_load = load(6, gain_hbm, gain_ref)
+    ranges_load = load(7, ranges_hbm, ranges_ref)
+    ids_load = load(8, ids_hbm, ids_ref)
+    absorb_load = load(9, absorb_hbm, absorb_w)
+
+    def other(k):
+        place = lax.rem(me * mp_count + my_mp + k, seq_count * mp_count)
+        return (place // mp_count, lax.rem(place, mp_count))
+
+    device_count = seq_count * mp_count
     barrier = pltpu.get_barrier_semaphore()
-    for k in range(1, seq_count):
+    for k in range(1, device_count):
         pl.semaphore_signal(
-            barrier, inc=1, device_id=(seq_peer(k), my_mp), device_id_type=pl.DeviceIdType.MESH
-        )
-    for k in range(1, mp_count):
-        pl.semaphore_signal(
-            barrier, inc=1, device_id=(me, mp_peer(k)), device_id_type=pl.DeviceIdType.MESH
-        )
+            barrier, inc=1, device_id=other(k), device_id_type=pl.DeviceIdType.MESH
+        )
+    keep_load.wait()
+    drop_load.wait()
 
     keep = jnp.concatenate([keep_ref[:, 0, :], keep_ref[:, 0, :]], axis=1).astype(F32)
     keep_t = jnp.transpose(keep)[:KB]
@@ -349,14 +368,15 @@
         pick = jnp.where(jnp.broadcast_to(keep_t[:, r : r + 1], (KB, BLK)) == position, 1.0, 0.0)
         flag = jnp.sum(pick, axis=0, keepdims=True)
         kept_flag = jnp.where(request_sub == r, jnp.broadcast_to(flag, (RQ, BLK)), kept_flag)
-        picks.append(pick.astype(BF16))
+        picks.append(pick)
     dropped = drop_ref[...].astype(F32) * (1.0 - kept_flag)
     mass = jnp.sum(dropped, axis=1, keepdims=True)
 
+    hidden_load.wait()
     query_load.wait()
     query = jnp.dot(hidden_ref[...], query_w[...], preferred_element_type=F32)
     query_recv[me] = fold(query).astype(BF16)
-    pl.semaphore_wait(barrier, seq_count + mp_count - 2)
+    pl.semaphore_wait(barrier, device_count - 1)
     query_copies = [
         to_peer(
             query_recv.at[me],
@@ -367,15 +387,19 @@
         )
         for k in range(1, seq_count)
     ]
-    out_load = load(3, out_hbm, out_w)
-    up_load = load(4, up_hbm.at[pl.ds(me * 2, 2)], up_w)
-    head_load = load(5, head_hbm, head_w)
+    out_load = load(10, out_hbm, out_w)
+    up_load = load(11, up_hbm.at[pl.ds(me * 2, 2)], up_w)
+    head_load = load(12, head_hbm, head_w)
 
     cache_load.wait()
     summed = jnp.zeros((PAIR, row_width), F32)
     pad = jnp.zeros((PAIR - RQ, BLK), F32)
     for r in range(RQ):
-        chosen = lax.dot_general(picks[r], cache[r], contract, preferred_element_type=F32)
+        own = jnp.where(request_sub == r, dropped, 0.0)
+        both = jnp.concatenate([picks[r], own, pad], axis=0).astype(BF16)
+        chosen = lax.dot_general(both, cache[r], contract, preferred_element_type=F32)
+        summed = summed + chosen[KB:]
+        chosen = chosen[:KB]
         kept[r] = chosen.astype(BF16)
         for i in range(LAT // LANES):
             piece = chosen[:, i * LANES : (i + 1) * LANES]
@@ -383,9 +407,6 @@
         rope = chosen[:, LAT:]
         rope = jnp.concatenate([rope[: KB // 2], rope[KB // 2 :]], axis=1)
         blocks[r, ROPE_AT:SUMM_AT, :] = rope.astype(BF16)
-        own = jnp.where(request_sub == r, dropped, 0.0)
-        own = jnp.concatenate([own, pad], axis=0).astype(BF16)
-        summed = summed + lax.dot_general(own, cache[r], contract, preferred_element_type=F32)
     mass_pair = jnp.concatenate([mass, jnp.ones_like(mass)], axis=0)
     summary = (summed / mass_pair).astype(BF16)
     summ[...] = summary
@@ -401,6 +422,7 @@
             lines = jnp.where(line == i, jnp.broadcast_to(piece, (PAIR, LANES)), lines)
         blocks[r, SUMM_AT:, :] = lines.astype(BF16)
 
+    dest_load.wait()
     owners = [dest_ref[r, me] >> 2 for r in range(RQ)]
 
     def request_for(owner):
@@ -425,6 +447,8 @@
     absorb_load.wait()
     for copy in query_copies:
         copy.wait_recv()
+    early = (1, seq_count - 1)
+    pack_copies = [start_pack(k) for k in early]
     first_half = lax.broadcasted_iota(jnp.int32, (PAIR, NOPE), 0) < RQ
     for s in range(seq_count):
         part = query_recv[s]
@@ -486,6 +510,8 @@
     ]
     part_recv[me] = part_send[me]
 
+    ranges_load.wait()
+    ids_load.wait()
     total_rows = mp_count * RQ
     window_row = lax.broadcasted_iota(jnp.int32, (total_rows, 128), 0)
     window_low = jnp.zeros((total_rows, 128), jnp.int32)
@@ -508,7 +534,7 @@
     up_load.wait()
     for copy in part_copies:
         copy.wait_recv()
-    pack_copies = [start_pack(k) for k in range(1, seq_count)]
+    pack_copies += [start_pack(k) for k in range(1, seq_count) if k not in early]
     levels = [
         jnp.sum(part_recv[s, :, LAT:].astype(F32), axis=1, keepdims=True)
         for s in range(seq_count)
@@ -546,6 +572,13 @@
     hidden = residual.astype(F32) + jnp.dot(all_values, out_w[...], preferred_element_type=F32)
     hidden = hidden.astype(BF16)
     hidden_out[...] = hidden
+
+    def store(i, src, dst):
+        copy = pltpu.make_async_copy(src, dst, store_sem.at[i])
+        copy.start()
+        return copy
+
+    stores = [store(0, hidden_out, hidden_out_hbm)]
     hidden_all[my_mp, me] = fold(hidden.astype(F32)).astype(BF16)
 
     hidden_copies = [
@@ -575,6 +608,8 @@
     )
     own_norm = jnp.sqrt(jnp.mean(own_rows * own_rows, axis=1, keepdims=True))
     norm_out[...] = as_row(own_norm)
+    stores.append(store(1, norm_out, norm_hbm))
+    gain_load.wait()
     gain = gain_ref[...].astype(F32).reshape(1, -1)
     for copy in group_copies:
         copy.wait_recv()
@@ -603,30 +638,14 @@
         0, vocab_width // tile, head_step, jnp.full((total_rows, 128), NEGATIVE, F32)
     )
     best = jnp.broadcast_to(jnp.max(best, axis=1, keepdims=True), (total_rows, 128))
-    mp_best[...] = best.reshape(mp_count, RQ, 128)
-    mp_best_recv[my_mp] = mp_best[my_mp]
+    diagonal = window_row == lane
+    here = me * mp_count + my_mp
+    best_all[here] = jnp.sum(jnp.where(diagonal, best, 0.0), axis=0, keepdims=True)
     best_copies = [
         to_peer(
-            mp_best.at[mp_peer(k)],
-            mp_best_recv.at[my_mp],
-            a_send.at[k - 1],
-            a_recv.at[k - 1],
-            (me, mp_peer(k)),
-        )
-        for k in range(1, mp_count)
-    ]
-    for copy in best_copies:
-        copy.wait_recv()
-    seq_best[me] = jnp.max(mp_best_recv[...], axis=0)
-    last_copies = [
-        to_peer(
-            seq_best.at[me],
-            seq_best.at[me],
-            b_send.at[k - 1],
-            b_recv.at[k - 1],
-            (seq_peer(k), my_mp),
-        )
-        for k in range(1, seq_count)
+            best_all.at[here], best_all.at[here], b_send.at[k - 1], b_recv.at[k - 1], other(k)
+        )
+        for k in range(1, device_count)
     ]
 
     for copy in pack_copies:
@@ -644,10 +663,17 @@
         line = jnp.concatenate([tail[i : i + 1] for i in range(5)], axis=1)
         lines.append(line[:, :row_width])
     summary_out[...] = jnp.concatenate(lines, axis=0).astype(BF16)
-
-    for copy in last_copies:
+    stores.append(store(2, rows_out, rows_hbm))
+    stores.append(store(3, summary_out, summary_hbm))
+
+    for copy in best_copies:
         copy.wait_recv()
-    top_out[...] = as_row(jnp.max(seq_best[...], axis=0))
+    top = jnp.max(best_all[...], axis=0)
+    own_top = top[:, :RQ]
+    for m in range(1, mp_count):
+        own_top = jnp.where(my_mp == m, top[:, m * RQ : (m + 1) * RQ], own_top)
+    top_out[...] = own_top
+    stores.append(store(4, top_out, top_hbm))
     for copy in (
         query_copies
         + pack_copies
@@ -656,9 +682,10 @@
         + hidden_copies
         + group_copies
         + best_copies
-        + last_copies
     ):
         copy.wait_send()
+    for copy in stores:
+        copy.wait()
 
 
 def publish_kernel(*refs):
@@ -695,10 +722,9 @@
     slot_count = RQ // 2
     depth, vocab_width = head_weight.shape
     tile = next(t for t in (640, 512, 384, 256, 128) if vocab_width % t == 0)
-    vmem = pl.BlockSpec(memory_space=pltpu.VMEM)
-    smem = pl.BlockSpec(memory_space=pltpu.SMEM)
     hbm = pl.BlockSpec(memory_space=pltpu.HBM)
     seq_sems = pltpu.SemaphoreType.DMA((seq_count - 1,))
+    all_sems = pltpu.SemaphoreType.DMA((seq_count * mp_count - 1,))
     mp_sems = pltpu.SemaphoreType.DMA((mp_count - 1,))
     outs = pl.pallas_call(
         functools.partial(layer_kernel, seq_count, mp_count, vocab_width, tile),
@@ -709,9 +735,21 @@
             jax.ShapeDtypeStruct((1, RQ), F32),
             jax.ShapeDtypeStruct((1, RQ), F32),
         ),
-        in_specs=[vmem] * 4 + [smem] * 3 + [hbm] * 6,
-        out_specs=(vmem,) * 5,
+        in_specs=[hbm] * 13,
+        out_specs=(hbm,) * 5,
         scratch_shapes=[
+            pltpu.VMEM(hidden_in.shape, BF16),
+            pltpu.VMEM(keep_lists.shape, jnp.int32),
+            pltpu.VMEM(drop_weights.shape, jnp.int32),
+            pltpu.VMEM(final_gain.shape, BF16),
+            pltpu.SMEM(pack_dest.shape, jnp.int32),
+            pltpu.SMEM((2, TENANTS), jnp.int32),
+            pltpu.SMEM(tenant_ids.shape, jnp.int32),
+            pltpu.VMEM((slot_count, KB, row_width), BF16),
+            pltpu.VMEM((slot_count, row_width), BF16),
+            pltpu.VMEM((RQ, out_weight.shape[1]), BF16),
+            pltpu.VMEM((1, RQ), F32),
+            pltpu.VMEM((1, RQ), F32),
             pltpu.VMEM(query_weight.shape, BF16),
             pltpu.VMEM(key_absorb.shape, BF16),
             pltpu.VMEM((2,) + value_up.shape[1:], BF16),
@@ -729,16 +767,15 @@
             pltpu.VMEM((seq_count, PAIR, LAT + 128), BF16),
             pltpu.VMEM((seq_count, PAIR, VH), BF16),
             pltpu.VMEM((mp_count, seq_count, PAIR, out_weight.shape[1] // 2), BF16),
-            pltpu.VMEM((mp_count, RQ, 128), F32),
-            pltpu.VMEM((mp_count, RQ, 128), F32),
-            pltpu.VMEM((seq_count, RQ, 128), F32),
-            pltpu.SemaphoreType.DMA((6,)),
+            pltpu.VMEM((seq_count * mp_count, 1, 128), F32),
+            pltpu.SemaphoreType.DMA((13,)),
+            pltpu.SemaphoreType.DMA((5,)),
         ]
         + [seq_sems] * 10
-        + [mp_sems] * 4
-        + [seq_sems] * 2,
+        + [mp_sems] * 2
+        + [all_sems] * 2,
         compiler_params=pltpu.CompilerParams(
-            collective_id=0, has_side_effects=True, vmem_limit_bytes=213 * 2**18
+            collective_id=0, has_side_effects=True, vmem_limit_bytes=60 * 2**20
         ),
     )(
         hidden_in,
@@ -758,9 +795,10 @@
     outs = pl.pallas_call(
         publish_kernel,
         out_shape=tuple(jax.ShapeDtypeStruct(out.shape, out.dtype) for out in outs),
-        in_specs=[vmem] * 5,
+        in_specs=[hbm] * 5,
         out_specs=(hbm,) * 5,
         scratch_shapes=[pltpu.SemaphoreType.DMA((5,))],
+        compiler_params=pltpu.CompilerParams(vmem_limit_bytes=60 * 2**20),
     )(*outs)
     packed_rows, packed_summary, hidden_out, state_norm, top_logit = outs
     return (

time: 59.4 us -> 60.6 us (1.020)
  Pallas kernels: 50.5 us -> 59.8 us
  local copies, waits for them, and re-layouts: 7.79 us -> 0 us
    pallas_call x1, Pallas kernels: 1.77 us -> 11.4 us  [fused_body(): pl.pallas_call(publish_kernel, out_shape=tuple((jax.ShapeDtypeStruct(out....]
    unnamed x24 -> x0, local copies, waits for them, and re-layouts: 7.79 us -> none
where the time goes in v3:
time: 60.6 us; the launch traced here: 60.4 us
  Pallas kernels  59.8 us (99%)
  between operations  0.64 us (1%)
    pallas_call x1, Pallas kernels, fused_body(): pl.pallas_call(functools.partial(layer_kernel, seq_count, mp_count, vocab...  48.4 us
    pallas_call x1, Pallas kernels, fused_body(): pl.pallas_call(publish_kernel, out_shape=tuple((jax.ShapeDtypeStruct(out....  11.4 us

profile of v3, /device:TPU:0, one launch (start us, length us, event | category | flops | bytes accessed | tf_op | source)
XLA Modules:
  0.0 60.4 jit_solution(16041035938234390970)
XLA Ops:
  0.6 48.4 %shard_map.164 = (bf16[4,64,576]{2,1,0:T(8,128)(2,1)}, bf16[4,576]{1,0:T(4,128)(2,1)}, bf16[8,256]{1,0:T(8,128)(2,1)}, f32[1,8]{1,0:T(1,128)}, f32[1,8]{1,0:T(1,128)}) custom-call(bf16[8,2048]{1,0:T(8,128)(2,1)} %hidden_hbm.1, s32[8,1,64]{2,1,0:T(1,128)} %keep_hbm.1, s32[8,128]{1,0:T(8,128)} %drop_hbm.1, bf16[2048]{0:T(1024)(128)(2,1)} %gain_hbm.1, ...), custom_call_target="tpu_custom_call" | custom-call | tf_op jit(solution)/shard_map/pallas_call | solution.py:729
  49.0 11.4 %shard_map.165 = (bf16[4,64,576]{2,1,0:T(8,128)(2,1)}, bf16[4,576]{1,0:T(4,128)(2,1)}, bf16[8,256]{1,0:T(8,128)(2,1)}, f32[1,8]{1,0:T(1,128)}, f32[1,8]{1,0:T(1,128)}) custom-call(bf16[4,64,576]{2,1,0:T(8,128)(2,1)} %get-tuple-element.15.refs_0_, bf16[4,576]{1,0:T(4,128)(2,1)} %get-tuple-element.16.refs_1_, bf16[8,256]{1,0:T(8,128)(2,1)} %get-tuple-element.17.refs_2_, ...), custom_call_target="tpu_custom_call" | custom-call | tf_op jit(solution)/shard_map/pallas_call | solution.py:795

commit v4 on v3

--- a/solution.py
+++ b/solution.py
@@ -444,11 +444,13 @@
             (seq_peer(k), my_mp),
         )
 
+    far = seq_count // 2
+    lots = ((far, 1, seq_count - 1), (2,), tuple(range(3, far)) + tuple(range(far + 1, seq_count - 1)))
+    pack_copies = [start_pack(k) for k in lots[0]]
+
     absorb_load.wait()
     for copy in query_copies:
         copy.wait_recv()
-    early = (1, seq_count - 1)
-    pack_copies = [start_pack(k) for k in early]
     first_half = lax.broadcasted_iota(jnp.int32, (PAIR, NOPE), 0) < RQ
     for s in range(seq_count):
         part = query_recv[s]
@@ -534,7 +536,7 @@
     up_load.wait()
     for copy in part_copies:
         copy.wait_recv()
-    pack_copies += [start_pack(k) for k in range(1, seq_count) if k not in early]
+    pack_copies += [start_pack(k) for k in lots[1]]
     levels = [
         jnp.sum(part_recv[s, :, LAT:].astype(F32), axis=1, keepdims=True)
         for s in range(seq_count)
@@ -613,6 +615,7 @@
     gain = gain_ref[...].astype(F32).reshape(1, -1)
     for copy in group_copies:
         copy.wait_recv()
+    pack_copies += [start_pack(k) for k in lots[2]]
     normed = []
     for m in range(mp_count):
         group = jnp.concatenate([unfold(hidden_all[m, s]) for s in range(seq_count)], axis=1)
@@ -689,14 +692,22 @@
 
 
 def publish_kernel(*refs):
-    results, places, sem = refs[:5], refs[5:10], refs[10]
-    copies = [
-        pltpu.make_async_copy(result, place, sem.at[i])
-        for i, (result, place) in enumerate(zip(results, places))
+    results, places, staged = refs[:5], refs[5:10], refs[10:15]
+    in_sem, out_sem = refs[15:]
+    loads = [
+        pltpu.make_async_copy(result, stage, in_sem.at[i])
+        for i, (result, stage) in enumerate(zip(results, staged))
     ]
-    for copy in copies:
+    stores = [
+        pltpu.make_async_copy(stage, place, out_sem.at[i])
+        for i, (stage, place) in enumerate(zip(staged, places))
+    ]
+    for copy in loads:
         copy.start()
-    for copy in copies:
+    for load, store in zip(loads, stores):
+        load.wait()
+        store.start()
+    for copy in stores:
         copy.wait()
 
 
@@ -797,7 +808,8 @@
         out_shape=tuple(jax.ShapeDtypeStruct(out.shape, out.dtype) for out in outs),
         in_specs=[hbm] * 5,
         out_specs=(hbm,) * 5,
-        scratch_shapes=[pltpu.SemaphoreType.DMA((5,))],
+        scratch_shapes=[pltpu.VMEM(out.shape, out.dtype) for out in outs]
+        + [pltpu.SemaphoreType.DMA((5,))] * 2,
         compiler_params=pltpu.CompilerParams(vmem_limit_bytes=60 * 2**20),
     )(*outs)
     packed_rows, packed_summary, hidden_out, state_norm, top_logit = outs

time: 60.6 us -> 46.9 us (0.77)
  Pallas kernels: 59.8 us -> 46 us
    pallas_call x1, Pallas kernels: 11.4 us -> 1.79 us  [fused_body(): pl.pallas_call(publish_kernel, out_shape=tuple((jax.ShapeDtypeStruct(out....]
    pallas_call x1, Pallas kernels: 48.4 us -> 44.2 us  [fused_body(): pl.pallas_call(functools.partial(layer_kernel, seq_count, mp_count, vocab...]
where the time goes in v4:
time: 46.9 us; the launch traced here: 46.7 us
  Pallas kernels  46 us (98%)
  between operations  0.64 us (1%)
    pallas_call x1, Pallas kernels, fused_body(): pl.pallas_call(functools.partial(layer_kernel, seq_count, mp_count, vocab...  44.2 us
    pallas_call x1, Pallas kernels, fused_body(): pl.pallas_call(publish_kernel, out_shape=tuple((jax.ShapeDtypeStruct(out....  1.79 us

profile of v4, /device:TPU:0, one launch (start us, length us, event | category | flops | bytes accessed | tf_op | source)
XLA Modules:
  0.0 46.7 jit_solution(16166801423578303182)
XLA Ops:
  0.6 44.2 %shard_map.164 = (bf16[4,64,576]{2,1,0:T(8,128)(2,1)}, bf16[4,576]{1,0:T(4,128)(2,1)}, bf16[8,256]{1,0:T(8,128)(2,1)}, f32[1,8]{1,0:T(1,128)}, f32[1,8]{1,0:T(1,128)}) custom-call(bf16[8,2048]{1,0:T(8,128)(2,1)} %hidden_hbm.1, s32[8,1,64]{2,1,0:T(1,128)} %keep_hbm.1, s32[8,128]{1,0:T(8,128)} %drop_hbm.1, bf16[2048]{0:T(1024)(128)(2,1)} %gain_hbm.1, ...), custom_call_target="tpu_custom_call" | custom-call | tf_op jit(solution)/shard_map/pallas_call | solution.py:740
  44.9 1.8 %shard_map.165 = (bf16[4,64,576]{2,1,0:T(8,128)(2,1)}, bf16[4,576]{1,0:T(4,128)(2,1)}, bf16[8,256]{1,0:T(8,128)(2,1)}, f32[1,8]{1,0:T(1,128)}, f32[1,8]{1,0:T(1,128)}) custom-call(bf16[4,64,576]{2,1,0:T(8,128)(2,1)} %get-tuple-element.15.refs_0_, bf16[4,576]{1,0:T(4,128)(2,1)} %get-tuple-element.16.refs_1_, bf16[8,256]{1,0:T(8,128)(2,1)} %get-tuple-element.17.refs_2_, ...), custom_call_target="tpu_custom_call" | custom-call | tf_op jit(solution)/shard_map/pallas_call | solution.py:806

commit v5 on v4

--- a/solution.py
+++ b/solution.py
@@ -445,8 +445,8 @@
         )
 
     far = seq_count // 2
-    lots = ((far, 1, seq_count - 1), (2,), tuple(range(3, far)) + tuple(range(far + 1, seq_count - 1)))
-    pack_copies = [start_pack(k) for k in lots[0]]
+    early = (far, 1, seq_count - 1)
+    pack_copies = [start_pack(k) for k in early]
 
     absorb_load.wait()
     for copy in query_copies:
@@ -536,7 +536,6 @@
     up_load.wait()
     for copy in part_copies:
         copy.wait_recv()
-    pack_copies += [start_pack(k) for k in lots[1]]
     levels = [
         jnp.sum(part_recv[s, :, LAT:].astype(F32), axis=1, keepdims=True)
         for s in range(seq_count)
@@ -615,7 +614,7 @@
     gain = gain_ref[...].astype(F32).reshape(1, -1)
     for copy in group_copies:
         copy.wait_recv()
-    pack_copies += [start_pack(k) for k in lots[2]]
+    pack_copies += [start_pack(k) for k in range(1, seq_count) if k not in early]
     normed = []
     for m in range(mp_count):
         group = jnp.concatenate([unfold(hidden_all[m, s]) for s in range(seq_count)], axis=1)

time: 46.9 us -> 47.6 us (1.015)
  Pallas kernels: 46 us -> 46.8 us
    pallas_call x1, Pallas kernels: 44.2 us -> 45 us  [fused_body(): pl.pallas_call(functools.partial(layer_kernel, seq_count, mp_count, vocab...]
where the time goes in v5:
time: 47.6 us; the launch traced here: 47.5 us
  Pallas kernels  46.8 us (98%)
  between operations  0.64 us (1%)
    pallas_call x1, Pallas kernels, fused_body(): pl.pallas_call(functools.partial(layer_kernel, seq_count, mp_count, vocab...  45 us
    pallas_call x1, Pallas kernels, fused_body(): pl.pallas_call(publish_kernel, out_shape=tuple((jax.ShapeDtypeStruct(out....  1.79 us

profile of v5, /device:TPU:0, one launch (start us, length us, event | category | flops | bytes accessed | tf_op | source)
XLA Modules:
  0.0 47.5 jit_solution(13544645085815216295)
XLA Ops:
  0.6 45.0 %shard_map.164 = (bf16[4,64,576]{2,1,0:T(8,128)(2,1)}, bf16[4,576]{1,0:T(4,128)(2,1)}, bf16[8,256]{1,0:T(8,128)(2,1)}, f32[1,8]{1,0:T(1,128)}, f32[1,8]{1,0:T(1,128)}) custom-call(bf16[8,2048]{1,0:T(8,128)(2,1)} %hidden_hbm.1, s32[8,1,64]{2,1,0:T(1,128)} %keep_hbm.1, s32[8,128]{1,0:T(8,128)} %drop_hbm.1, bf16[2048]{0:T(1024)(128)(2,1)} %gain_hbm.1, ...), custom_call_target="tpu_custom_call" | custom-call | tf_op jit(solution)/shard_map/pallas_call | solution.py:739
  45.7 1.8 %shard_map.165 = (bf16[4,64,576]{2,1,0:T(8,128)(2,1)}, bf16[4,576]{1,0:T(4,128)(2,1)}, bf16[8,256]{1,0:T(8,128)(2,1)}, f32[1,8]{1,0:T(1,128)}, f32[1,8]{1,0:T(1,128)}) custom-call(bf16[4,64,576]{2,1,0:T(8,128)(2,1)} %get-tuple-element.15.refs_0_, bf16[4,576]{1,0:T(4,128)(2,1)} %get-tuple-element.16.refs_1_, bf16[8,256]{1,0:T(8,128)(2,1)} %get-tuple-element.17.refs_2_, ...), custom_call_target="tpu_custom_call" | custom-call | tf_op jit(solution)/shard_map/pallas_call | solution.py:805
